TPU v7x, 32 devices: a whole 2x2x4 slice. The times are simulated.
32 devices in a mesh: dp: 8 (over y, x, core), tensor: 4 (over z).
Axes of the slice: x: 2, y: 2, z: 4, core: 2. Of those that a mesh axis runs over, the one named last changes fastest.
Arguments:
- tokens: bfloat16 [5120, 2048], P(('dp', 'tensor')), may hold values from -6 to 6
- lengths: int32 [8, 3], P('dp'), may hold values from 1 to 512, 640 in all within a row
- attn_gain: bfloat16 [2048], P('dp'), may hold values from 0.5 to 1.5
- w_query: bfloat16 [2048, 2048], P('dp', 'tensor'), may hold values from -0.125 to 0.125
- w_key: bfloat16 [2048, 256], P('dp', 'tensor'), may hold values from -0.125 to 0.125
- w_value: bfloat16 [2048, 256], P('dp', 'tensor'), may hold values from -0.125 to 0.125
- w_output: bfloat16 [2048, 2048], P('tensor', 'dp'), may hold values from -2 to 2
- ffn_gain: bfloat16 [2048], P('dp'), may hold values from 0.5 to 1.5
- w_gate: bfloat16 [2048, 5632], P('dp', 'tensor'), may hold values from -0.125 to 0.125
- w_up: bfloat16 [2048, 5632], P('dp', 'tensor'), may hold values from -0.125 to 0.125
- w_down: bfloat16 [5632, 2048], P('tensor', 'dp'), may hold values from -0.078125 to 0.078125
- cotangent: bfloat16 [5120, 2048], P(('dp', 'tensor')), may hold values from -6 to 6
Outputs:
- block_out: bfloat16 [5120, 2048], P(('dp', 'tensor'))
- grad_tokens: bfloat16 [5120, 2048], P(('dp', 'tensor'))
- grad_attn_gain: float32 [2048], P('dp')
- grad_query: float32 [2048, 2048], P('dp', 'tensor')
- grad_key: float32 [2048, 256], P('dp', 'tensor')
- grad_value: float32 [2048, 256], P('dp', 'tensor')
- grad_output: float32 [2048, 2048], P('tensor', 'dp')
- grad_ffn_gain: float32 [2048], P('dp')
- grad_gate: float32 [2048, 5632], P('dp', 'tensor')
- grad_up: float32 [2048, 5632], P('dp', 'tensor')
- grad_down: float32 [5632, 2048], P('tensor', 'dp')
Inputs may be any that keep to these rules, and one draw needn't show every extreme that they name: Each row lists the lengths of the sequences packed in order into one group of 640 tokens; a row sums to 640 and its largest entry is exactly 512.
All inputs are finite; a program needn't handle non-finite values.
Results may differ from a plain program's by a relative error of at most 0.025.
Values may be sent and summed in bfloat16 or wider, within the bound.
No kernel may reach another device: no remote copies, remote signals or barrier semaphores. Data moves between devices by JAX's collectives and lax.ppermute only.
A program may use at most 192 MiB of HBM per device.

v0:
```python
import math

import jax
import jax.numpy as jnp
from jax import lax
from jax.sharding import PartitionSpec as P

HEAD_DIM = 64


EPS = 1e-05
ROPE_BASE = 10000.0
NEG_FILL = -1e30


def seq_layout(row_lengths, total):
    places = jnp.arange(total, dtype=jnp.int32)
    ends = jnp.cumsum(row_lengths)
    starts = ends - row_lengths
    segment = jnp.sum((places[:, None] >= ends[None, :]).astype(jnp.int32), axis=1)
    owner = segment[:, None] == jnp.arange(row_lengths.shape[0], dtype=jnp.int32)[None, :]
    begin = jnp.sum(jnp.where(owner, starts[None, :], 0), axis=1)
    return (segment, places - begin)


def rope_tables(position, head_dim):
    half = head_dim // 2
    freqs = ROPE_BASE ** (-(jnp.arange(half, dtype=jnp.float32) * 2.0 / head_dim))
    angles = position.astype(jnp.float32)[:, None] * freqs[None, :]
    cosine = jnp.cos(angles)
    sine = jnp.sin(angles)
    return (jnp.concatenate([cosine, cosine], 1), jnp.concatenate([sine, sine], 1))


def rotate(values, cosine, sine):
    half = values.shape[-1] // 2
    turned = jnp.concatenate([-values[..., half:], values[..., :half]], -1)
    return values * cosine[:, None, :] + turned * sine[:, None, :]


def unrotate(grads, cosine, sine):
    half = grads.shape[-1] // 2
    scaled = grads * sine[:, None, :]
    back = jnp.concatenate([scaled[..., half:], -scaled[..., :half]], -1)
    return grads * cosine[:, None, :] + back


def inner(left, right):
    return lax.dot_general(
        left, right, (((0,), (0,)), ((), ())), preferred_element_type=jnp.float32
    )


def outer_t(left, right):
    return lax.dot_general(
        left, right, (((1,), (1,)), ((), ())), preferred_element_type=jnp.float32
    )


def norm_back(d_normed, unit, inv, gain):
    scaled = d_normed * gain
    return inv * (scaled - unit * jnp.mean(scaled * unit, -1, keepdims=True))


def body(
    tokens,
    lengths,
    attn_gain,
    w_query,
    w_key,
    w_value,
    w_output,
    ffn_gain,
    w_gate,
    w_up,
    w_down,
    cotangent,
):
    scale = 1.0 / math.sqrt(HEAD_DIM)
    local_rows = tokens.shape[0]
    group_rows = local_rows * lax.axis_size("tensor")
    block_rows = min(group_rows, 640)
    full_query, full_key, full_value, full_output, full_attn_gain = (
        lax.all_gather(w_query, "dp", axis=0, tiled=True),
        lax.all_gather(w_key, "dp", axis=0, tiled=True),
        lax.all_gather(w_value, "dp", axis=0, tiled=True),
        lax.all_gather(w_output, "dp", axis=1, tiled=True),
        lax.all_gather(attn_gain, "dp", axis=0, tiled=True),
    )
    kv_local = full_key.shape[1] // HEAD_DIM
    q_local = full_query.shape[1] // HEAD_DIM
    group = q_local // kv_local
    gain_one = full_attn_gain.astype(jnp.float32)
    resid = tokens.astype(jnp.float32)
    inv_one = lax.rsqrt(jnp.mean(resid * resid, -1, keepdims=True) + EPS)
    unit_one = resid * inv_one
    gathered_one = lax.all_gather(
        (unit_one * gain_one).astype(jnp.bfloat16), "tensor", axis=0, tiled=True
    )
    segment, position = seq_layout(lengths[0], group_rows)
    cosine, sine = rope_tables(position, HEAD_DIM)
    places = jnp.arange(group_rows, dtype=jnp.int32)
    query = jnp.dot(gathered_one, full_query, preferred_element_type=jnp.float32).reshape(
        group_rows, q_local, HEAD_DIM
    )
    query = (
        rotate(query, cosine, sine)
        .astype(jnp.bfloat16)
        .reshape(group_rows, kv_local, group, HEAD_DIM)
    )
    key = jnp.dot(gathered_one, full_key, preferred_element_type=jnp.float32).reshape(
        group_rows, kv_local, HEAD_DIM
    )
    key = rotate(key, cosine, sine).astype(jnp.bfloat16)
    value = (
        jnp.dot(gathered_one, full_value, preferred_element_type=jnp.float32)
        .astype(jnp.bfloat16)
        .reshape(group_rows, kv_local, HEAD_DIM)
    )

    def block_scores(index):
        first = index * block_rows
        last = first + block_rows
        scores = (
            jnp.einsum("qcgd,kcd->cgqk", query, key, preferred_element_type=jnp.float32) * scale
        )
        allowed = (segment[first:last, None] == segment[None, :last]) & (
            places[None, :last] <= places[first:last, None]
        )
        return (query, jnp.where(allowed[None, None], scores, NEG_FILL))

    index = 0
    last = (index + 1) * block_rows
    q_block, scores = block_scores(index)
    row_max = jnp.max(scores, -1, keepdims=True)
    raised = jnp.exp(scores - row_max)
    row_total = jnp.sum(raised, -1, keepdims=True)
    log_sums = [row_max + jnp.log(row_total)]
    prob = (raised / row_total).astype(jnp.bfloat16)
    pieces = jnp.einsum("cgqk,kcd->qcgd", prob, value, preferred_element_type=jnp.float32)
    attended = pieces.reshape(group_rows, q_local * HEAD_DIM).astype(jnp.bfloat16)
    rows = attended
    hidden = resid + lax.psum_scatter(
        jnp.dot(rows, full_output, preferred_element_type=jnp.float32).astype(jnp.bfloat16),
        "tensor",
        scatter_dimension=0,
        tiled=True,
    ).astype(jnp.float32)
    full_gate, full_up, full_down, full_ffn_gain = (
        lax.all_gather(w_gate, "dp", axis=0, tiled=True),
        lax.all_gather(w_up, "dp", axis=0, tiled=True),
        lax.all_gather(w_down, "dp", axis=1, tiled=True),
        lax.all_gather(ffn_gain, "dp", axis=0, tiled=True),
    )
    gain_two = full_ffn_gain.astype(jnp.float32)
    inv_two = lax.rsqrt(jnp.mean(hidden * hidden, -1, keepdims=True) + EPS)
    unit_two = hidden * inv_two
    gathered_two = lax.all_gather(
        (unit_two * gain_two).astype(jnp.bfloat16), "tensor", axis=0, tiled=True
    )
    gate = jnp.dot(gathered_two, full_gate, preferred_element_type=jnp.float32)
    up_part = jnp.dot(gathered_two, full_up, preferred_element_type=jnp.float32)
    sigma = jax.nn.sigmoid(gate)
    swish = gate * sigma
    activation = (swish * up_part).astype(jnp.bfloat16)
    rows = activation
    block_out = (
        hidden
        + lax.psum_scatter(
            jnp.dot(rows, full_down, preferred_element_type=jnp.float32).astype(jnp.bfloat16),
            "tensor",
            scatter_dimension=0,
            tiled=True,
        ).astype(jnp.float32)
    ).astype(jnp.bfloat16)
    cot_full = lax.all_gather(cotangent, "tensor", axis=0, tiled=True)
    d_act = outer_t(cot_full, full_down)
    grad_down_local = inner(activation, cot_full)
    d_gate = (d_act * up_part * (sigma * (1.0 + gate * (1.0 - sigma)))).astype(jnp.bfloat16)
    d_up = (d_act * swish).astype(jnp.bfloat16)
    d_normed_two = lax.psum_scatter(
        (outer_t(d_gate, full_gate) + outer_t(d_up, full_up)).astype(jnp.bfloat16),
        "tensor",
        scatter_dimension=0,
        tiled=True,
    ).astype(jnp.float32)
    grad_gate_local = inner(gathered_two, d_gate)
    grad_up_local = inner(gathered_two, d_up)
    gain_two_part = jnp.sum(d_normed_two * unit_two, 0)
    d_hidden = cotangent.astype(jnp.float32) + norm_back(d_normed_two, unit_two, inv_two, gain_two)
    d_hidden_full = lax.all_gather(d_hidden.astype(jnp.bfloat16), "tensor", axis=0, tiled=True)
    grad_output_local = inner(attended, d_hidden_full)
    d_attended = (
        outer_t(d_hidden_full, full_output)
        .astype(jnp.bfloat16)
        .reshape(group_rows, kv_local, group, HEAD_DIM)
    )
    d_key = jnp.zeros((group_rows, kv_local, HEAD_DIM), jnp.float32)
    d_value = jnp.zeros((group_rows, kv_local, HEAD_DIM), jnp.float32)
    index = 0
    first = index * block_rows
    last = first + block_rows
    q_block, scores = block_scores(index)
    prob = jnp.exp(scores - log_sums[index])
    d_prob = jnp.einsum("qcgd,kcd->cgqk", d_attended, value, preferred_element_type=jnp.float32)
    delta = jnp.sum(prob * d_prob, -1, keepdims=True)
    d_scores = (prob * (d_prob - delta)).astype(jnp.bfloat16)
    d_query_parts = (
        jnp.einsum("cgqk,kcd->qcgd", d_scores, key, preferred_element_type=jnp.float32) * scale
    )
    key_part = (
        jnp.einsum("cgqk,qcgd->kcd", d_scores, q_block, preferred_element_type=jnp.float32) * scale
    )
    value_part = jnp.einsum(
        "cgqk,qcgd->kcd", prob.astype(jnp.bfloat16), d_attended, preferred_element_type=jnp.float32
    )
    d_key = d_key.at[:last].add(key_part)
    d_value = d_value.at[:last].add(value_part)
    d_query = d_query_parts.reshape(group_rows, q_local, HEAD_DIM)
    d_query = (
        unrotate(d_query, cosine, sine).reshape(group_rows, q_local * HEAD_DIM).astype(jnp.bfloat16)
    )
    d_key = (
        unrotate(d_key, cosine, sine).reshape(group_rows, kv_local * HEAD_DIM).astype(jnp.bfloat16)
    )
    d_value = d_value.reshape(group_rows, kv_local * HEAD_DIM).astype(jnp.bfloat16)
    total = outer_t(d_query, full_query) + outer_t(d_key, full_key)
    d_normed_one = lax.psum_scatter(
        (total + outer_t(d_value, full_value)).astype(jnp.bfloat16),
        "tensor",
        scatter_dimension=0,
        tiled=True,
    ).astype(jnp.float32)
    grad_query_local = inner(gathered_one, d_query)
    grad_key_local = inner(gathered_one, d_key)
    grad_value_local = inner(gathered_one, d_value)
    gain_one_part = jnp.sum(d_normed_one * unit_one, 0)
    grad_tokens = (d_hidden + norm_back(d_normed_one, unit_one, inv_one, gain_one)).astype(
        jnp.bfloat16
    )
    (
        grad_query,
        grad_key,
        grad_value,
        grad_output,
        gain_one_sum,
        grad_gate,
        grad_up,
        grad_down,
        gain_two_sum,
    ) = (
        lax.psum_scatter(
            grad_query_local.astype(jnp.bfloat16), "dp", scatter_dimension=0, tiled=True
        ).astype(jnp.float32),
        lax.psum_scatter(
            grad_key_local.astype(jnp.bfloat16), "dp", scatter_dimension=0, tiled=True
        ).astype(jnp.float32),
        lax.psum_scatter(
            grad_value_local.astype(jnp.bfloat16), "dp", scatter_dimension=0, tiled=True
        ).astype(jnp.float32),
        lax.psum_scatter(
            grad_output_local.astype(jnp.bfloat16), "dp", scatter_dimension=1, tiled=True
        ).astype(jnp.float32),
        lax.psum_scatter(
            gain_one_part.astype(jnp.bfloat16), "dp", scatter_dimension=0, tiled=True
        ).astype(jnp.float32),
        lax.psum_scatter(
            grad_gate_local.astype(jnp.bfloat16), "dp", scatter_dimension=0, tiled=True
        ).astype(jnp.float32),
        lax.psum_scatter(
            grad_up_local.astype(jnp.bfloat16), "dp", scatter_dimension=0, tiled=True
        ).astype(jnp.float32),
        lax.psum_scatter(
            grad_down_local.astype(jnp.bfloat16), "dp", scatter_dimension=1, tiled=True
        ).astype(jnp.float32),
        lax.psum_scatter(
            gain_two_part.astype(jnp.bfloat16), "dp", scatter_dimension=0, tiled=True
        ).astype(jnp.float32),
    )
    grad_attn_gain, grad_ffn_gain = lax.psum((gain_one_sum, gain_two_sum), "tensor")
    return (
        block_out,
        grad_tokens,
        grad_attn_gain,
        grad_query,
        grad_key,
        grad_value,
        grad_output,
        grad_ffn_gain,
        grad_gate,
        grad_up,
        grad_down,
    )


def solution(mesh):
    return jax.shard_map(
        body,
        mesh=mesh,
        in_specs=(
            P(("dp", "tensor"), None),
            P("dp", None),
            P("dp"),
            P("dp", "tensor"),
            P("dp", "tensor"),
            P("dp", "tensor"),
            P("tensor", "dp"),
            P("dp"),
            P("dp", "tensor"),
            P("dp", "tensor"),
            P("tensor", "dp"),
            P(("dp", "tensor"), None),
        ),
        out_specs=(
            P(("dp", "tensor"), None),
            P(("dp", "tensor"), None),
            P("dp"),
            P("dp", "tensor"),
            P("dp", "tensor"),
            P("dp", "tensor"),
            P("tensor", "dp"),
            P("dp"),
            P("dp", "tensor"),
            P("dp", "tensor"),
            P("tensor", "dp"),
        ),
        check_vma=False,
    )
```

profile of v0, /device:TPU:0, one launch (start us, length us, event | category | flops | bytes accessed | tf_op | source)
XLA Modules:
  0.0 1046.8 jit_solution(5258025392442520261)
XLA Ops:
  9.2 10.4 all-gather
  24.7 9.8 all_gather.42
  34.6 8.8 all_gather.41
  44.4 32.6 %all-gather.12.cloned.1.call-done = bf16[640,2048]{1,0:T(8,128)(2,1)} async-done(((bf16[160,2048]{1,0:T(8,128)(2,1)}), bf16[640,2048]{1,0:T(8,128)(2,1)}) %all-gather.12.cloned.1.call-update) | async-done | bytes 2621456 | tf_op jit(solution)/shard_map/all_gather | solution.py:97
  81.2 24.4 %all-gather.14.cloned.1.call-done = bf16[2048,512]{1,0:T(8,128)(2,1)} async-done(((bf16[256,512]{1,0:T(8,128)(2,1)}), bf16[2048,512]{1,0:T(8,128)(2,1)}) %all-gather.14.cloned.1.call-update) | async-done | bytes 2097168 | tf_op jit(solution)/shard_map/all_gather | solution.py:84
  123.2 12.5 %all-gather.16.cloned.1.call-done = bf16[512,2048]{1,0:T(8,128)(2,1)} async-done(((bf16[512,256]{1,0:T(8,128)(2,1)}), bf16[512,2048]{1,0:T(8,128)(2,1)}) %all-gather.16.cloned.1.call-update) | async-done | bytes 2097168 | tf_op jit(solution)/shard_map/all_gather | solution.py:87
  141.3 8.8 all-gather.1
  150.1 42.7 %reduce-scatter.12.cloned.1.call-done = bf16[160,2048]{1,0:T(8,128)(2,1)} async-done(((bf16[640,2048]{1,0:T(8,128)(2,1)}), bf16[160,2048]{1,0:T(8,128)(2,1)}) %reduce-scatter.12.cloned.1.call-update) | async-done | bytes 655376 | tf_op jit(solution)/shard_map/reduce_scatter | solution.py:143
  199.2 38.4 %all-gather.22.cloned.1.call-done = bf16[2048,1408]{1,0:T(8,128)(2,1)} async-done(((bf16[256,1408]{1,0:T(8,128)(2,1)}), bf16[2048,1408]{1,0:T(8,128)(2,1)}) %all-gather.22.cloned.1.call-update) | async-done | bytes 5767184 | tf_op jit(solution)/shard_map/all_gather | solution.py:151
  237.7 56.8 %all-gather.18.cloned.1.call-done = bf16[640,2048]{1,0:T(8,128)(2,1)} async-done(((bf16[160,2048]{1,0:T(8,128)(2,1)}), bf16[640,2048]{1,0:T(8,128)(2,1)}) %all-gather.18.cloned.1.call-update) | async-done | bytes 2621456 | tf_op jit(solution)/shard_map/all_gather | solution.py:158
  294.5 9.4 fusion.67
  303.9 34.6 %all-gather.20.cloned.1.call-done = bf16[2048,1408]{1,0:T(8,128)(2,1)} async-done(((bf16[256,1408]{1,0:T(8,128)(2,1)}), bf16[2048,1408]{1,0:T(8,128)(2,1)}) %all-gather.20.cloned.1.call-update) | async-done | bytes 5767184 | tf_op jit(solution)/shard_map/all_gather | solution.py:150
  338.5 9.4 fusion.66
  347.9 47.0 %all-gather.26.cloned.1.call-done = bf16[640,2048]{1,0:T(8,128)(2,1)} async-done(((bf16[160,2048]{1,0:T(8,128)(2,1)}), bf16[640,2048]{1,0:T(8,128)(2,1)}) %all-gather.26.cloned.1.call-update) | async-done | bytes 2621456 | tf_op jit(solution)/shard_map/all_gather | solution.py:176
  394.9 45.0 %all-gather.24.cloned.1.call-done = bf16[1408,2048]{1,0:T(8,128)(2,1)} async-done(((bf16[1408,256]{1,0:T(8,128)(2,1)}), bf16[1408,2048]{1,0:T(8,128)(2,1)}) %all-gather.24.cloned.1.call-update) | async-done | bytes 5767184 | tf_op jit(solution)/shard_map/all_gather | solution.py:152
  440.0 12.2 %multiply_convert_fusion = (bf16[640,1408]{1,0:T(8,128)(2,1)S(1)}, bf16[640,1408]{1,0:T(8,128)(2,1)S(1)}, bf16[640,1408]{1,0:T(8,128)(2,1)}) fusion(f32[640,1408]{1,0:T(8,128)} %fusion.66, f32[640,1408]{1,0:T(8,128)} %fusion.67, bf16[640,2048]{1,0:T(8,128)(2,1)} %all-gather.26.cloned.1.call-done, bf16[1408,2048]{1,0:T(8,128)(2,1)} %all-gather.24.cloned.1.call-done), kind=kOutput, calls=%fused_computation.22 | convolution fusion | flops 3704504320 | bytes 21004288 | tf_op jit(solution)/shard_map/dot_general | solution.py:55
  465.0 52.2 %reduce-scatter.16.cloned.1.call-done = bf16[160,2048]{1,0:T(8,128)(2,1)} async-done(((bf16[640,2048]{1,0:T(8,128)(2,1)}), bf16[160,2048]{1,0:T(8,128)(2,1)}) %reduce-scatter.16.cloned.1.call-update) | async-done | bytes 655376 | tf_op jit(solution)/shard_map/reduce_scatter | solution.py:181
  522.7 9.4 convolution_convert_fusion
  532.2 8.7 convolution_convert_fusion.1
  541.0 8.9 convolution_convert_fusion.2
  550.7 26.6 %all-gather.28.cloned.1.call-done = bf16[640,2048]{1,0:T(8,128)(2,1)} async-done(((bf16[160,2048]{1,0:T(8,128)(2,1)}), bf16[640,2048]{1,0:T(8,128)(2,1)}) %all-gather.28.cloned.1.call-update) | async-done | bytes 2621456 | tf_op jit(solution)/shard_map/all_gather | solution.py:191
  581.6 12.4 %fusion = (f32[8,640]{1,0:T(8,128)S(1)}, f32[640,640,8]{1,0,2:T(8,128)}) fusion(f32[1,8,640,640]{2,3,1,0:T(8,128)} %copy-done, f32[8,640]{1,0:T(8,128)S(1)} %log_add_fusion, bf16[640,64,1]{0,1,2:T(8,128)(2,1)S(1)} %copy-done.31, bf16[640,8,64]{0,2,1:T(8,128)(2,1)S(1)} %bitcast.172), kind=kOutput, calls=%fused_computation.3 | convolution fusion | flops 429255680 | bytes 26992640 | tf_op jit(solution)/shard_map/qcgd,kcd->cgqk/dot_general | solution.py:205
  647.7 53.7 %reduce-scatter.30.cloned.1.call-done = bf16[256,1408]{1,0:T(8,128)(2,1)} async-done(((bf16[2048,1408]{1,0:T(8,128)(2,1)}), bf16[256,1408]{1,0:T(8,128)(2,1)}) %reduce-scatter.30.cloned.1.call-update) | async-done | bytes 720912 | tf_op jit(solution)/shard_map/reduce_scatter | solution.py:270
  703.7 60.0 %reduce-scatter.28.cloned.1.call-done = bf16[256,1408]{1,0:T(8,128)(2,1)} async-done(((bf16[2048,1408]{1,0:T(8,128)(2,1)}), bf16[256,1408]{1,0:T(8,128)(2,1)}) %reduce-scatter.28.cloned.1.call-update) | async-done | bytes 720912 | tf_op jit(solution)/shard_map/reduce_scatter | solution.py:267
  766.0 35.1 %reduce-scatter.24.cloned.1.call-done = bf16[256,64]{0,1:T(8,128)(2,1)} async-done(((bf16[2048,64]{0,1:T(8,128)(2,1)}), bf16[256,64]{0,1:T(8,128)(2,1)}) %reduce-scatter.24.cloned.1.call-update) | async-done | bytes 32784 | tf_op jit(solution)/shard_map/reduce_scatter | solution.py:258
  802.5 35.7 %reduce-scatter.22.cloned.1.call-done = bf16[256,64]{0,1:T(8,128)(2,1)} async-done(((bf16[2048,64]{0,1:T(8,128)(2,1)}), bf16[256,64]{0,1:T(8,128)(2,1)}) %reduce-scatter.22.cloned.1.call-update) | async-done | bytes 32784 | tf_op jit(solution)/shard_map/reduce_scatter | solution.py:255
  839.6 43.4 %reduce-scatter.26.cloned.1.call-done = bf16[512,256]{1,0:T(8,128)(2,1)} async-done(((bf16[512,2048]{1,0:T(8,128)(2,1)}), bf16[512,256]{1,0:T(8,128)(2,1)}) %reduce-scatter.26.cloned.1.call-update) | async-done | bytes 262160 | tf_op jit(solution)/shard_map/reduce_scatter | solution.py:261
  884.7 42.6 %reduce-scatter.20.cloned.1.call-done = bf16[256,512]{1,0:T(8,128)(2,1)} async-done(((bf16[2048,512]{1,0:T(8,128)(2,1)}), bf16[256,512]{1,0:T(8,128)(2,1)}) %reduce-scatter.20.cloned.1.call-update) | async-done | bytes 262160 | tf_op jit(solution)/shard_map/reduce_scatter | solution.py:252
  929.1 52.7 %reduce-scatter.18.cloned.1.call-done = bf16[160,2048]{1,0:T(8,128)(2,1)} async-done(((bf16[640,2048]{1,0:T(8,128)(2,1)}), bf16[160,2048]{1,0:T(8,128)(2,1)}) %reduce-scatter.18.cloned.1.call-update) | async-done | bytes 655376 | tf_op jit(solution)/shard_map/reduce_scatter | solution.py:228
  983.5 13.8 %all-reduce.3 = (bf16[2048]{0:T(1024)(128)(2,1)S(1)}, bf16[2048]{0:T(1024)(128)(2,1)S(1)}) all-reduce(bf16[2048]{0:T(1024)(128)(2,1)S(1)} %get-tuple-element.53, bf16[2048]{0:T(1024)(128)(2,1)S(1)} %copy-done.38), channel_id=6, replica_groups=mesh['dp'=8,'tensor'=4] {'dp'}, use_global_device_ids=true, to_apply=%region_15.16.clone | all-reduce | flops 4096 | bytes 16384
  997.4 11.5 %all-reduce.2 = (f32[256]{0:T(256)}, f32[256]{0:T(256)}) all-reduce(f32[256]{0:T(256)S(1)} %get-tuple-element.86, f32[256]{0:T(256)S(1)} %get-tuple-element.85), channel_id=1, replica_groups=mesh['dp'=8,'tensor'=4] {'tensor'}, use_global_device_ids=true, to_apply=%region_16.17 | all-reduce | flops 512 | bytes 4096 | tf_op jit(solution)/shard_map/psum | solution.py:280
  1008.9 27.2 %reduce-scatter.14.cloned.1.call-done = bf16[160,2048]{1,0:T(8,128)(2,1)} async-done(((bf16[640,2048]{1,0:T(8,128)(2,1)}), bf16[160,2048]{1,0:T(8,128)(2,1)}) %reduce-scatter.14.cloned.1.call-update) | async-done | bytes 655376 | tf_op jit(solution)/shard_map/reduce_scatter | solution.py:169
  (216 shorter events, 133.8 us)
Async XLA Ops:
  7.2 27.4 %copy-start.37 = (bf16[256,64]{0,1:T(8,128)(2,1)S(1)}, bf16[256,64]{0,1:T(8,128)(2,1)}, u32[]{:S(2)}) copy-start(bf16[256,64]{0,1:T(8,128)(2,1)} %param.25) | copy-start | bytes 98308
  7.2 69.8 %all-gather.12.cloned.1.call-start = ((), (), s32[]{:S(2)}) async-start(), calls=%async_computation.11 | async-start | bytes 3276800 | tf_op jit(solution)/shard_map/all_gather | solution.py:97
  21.8 83.9 %all-gather.14.cloned.1.call-start = ((), (), s32[]{:S(2)}) async-start(), calls=%async_computation.12 | async-start | bytes 2359296 | tf_op jit(solution)/shard_map/all_gather | solution.py:84
  22.5 113.2 %all-gather.16.cloned.1.call-start = ((), (), s32[]{:S(2)}) async-start(), calls=%async_computation.13 | async-start | bytes 2359296 | tf_op jit(solution)/shard_map/all_gather | solution.py:87
  23.3 169.6 %reduce-scatter.12.cloned.1.call-start = ((), (), s32[]{:S(2)}) async-start(), calls=%async_computation.14 | async-start | bytes 3276800 | tf_op jit(solution)/shard_map/reduce_scatter | solution.py:143
  34.6 46.6 %copy-start.15 = (bf16[2048,64]{0,1:T(8,128)(2,1)}, bf16[2048,64]{0,1:T(8,128)(2,1)S(1)}, u32[]{:S(2)}) copy-start(bf16[2048,64]{0,1:T(8,128)(2,1)S(1)} %all_gather.42) | copy-start | bytes 786436
  43.4 67.6 %copy-start.13 = (bf16[2048,64]{0,1:T(8,128)(2,1)}, bf16[2048,64]{0,1:T(8,128)(2,1)S(1)}, u32[]{:S(2)}) copy-start(bf16[2048,64]{0,1:T(8,128)(2,1)S(1)} %all_gather.41) | copy-start | bytes 786436
  77.0 28.6 %copy-start.1 = (bf16[640,2048]{1,0:T(8,128)(2,1)S(1)}, bf16[640,2048]{1,0:T(8,128)(2,1)}, u32[]{:S(2)}) copy-start(bf16[640,2048]{1,0:T(8,128)(2,1)} %all-gather.12.cloned.1.call-done) | copy-start | bytes 7864324
  140.6 52.3 %copy-start.3 = (bf16[160,2048]{1,0:T(8,128)(2,1)S(1)}, bf16[160,2048]{1,0:T(8,128)(2,1)}, u32[]{:S(2)}) copy-start(bf16[160,2048]{1,0:T(8,128)(2,1)} %param.20) | copy-start | bytes 1966084
  140.6 97.0 %all-gather.22.cloned.1.call-start = ((), (), s32[]{:S(2)}) async-start(), calls=%async_computation.17 | async-start | bytes 6488064 | tf_op jit(solution)/shard_map/all_gather | solution.py:151
  141.2 153.3 %all-gather.18.cloned.1.call-start = ((), (), s32[]{:S(2)}) async-start(), calls=%async_computation.15 | async-start | bytes 3276800 | tf_op jit(solution)/shard_map/all_gather | solution.py:158
  196.5 142.0 %all-gather.20.cloned.1.call-start = ((), (), s32[]{:S(2)}) async-start(), calls=%async_computation.16 | async-start | bytes 6488064 | tf_op jit(solution)/shard_map/all_gather | solution.py:150
  197.2 197.7 %all-gather.26.cloned.1.call-start = ((), (), s32[]{:S(2)}) async-start(), calls=%async_computation.20 | async-start | bytes 3276800 | tf_op jit(solution)/shard_map/all_gather | solution.py:176
  198.0 242.0 %all-gather.24.cloned.1.call-start = ((), (), s32[]{:S(2)}) async-start(), calls=%async_computation.18 | async-start | bytes 6488064 | tf_op jit(solution)/shard_map/all_gather | solution.py:152
  198.7 318.5 %reduce-scatter.16.cloned.1.call-start = ((), (), s32[]{:S(2)}) async-start(), calls=%async_computation.21 | async-start | bytes 3276800 | tf_op jit(solution)/shard_map/reduce_scatter | solution.py:181
  464.9 112.4 %all-gather.28.cloned.1.call-start = ((), (), s32[]{:S(2)}) async-start(), calls=%async_computation.22 | async-start | bytes 3276800 | tf_op jit(solution)/shard_map/all_gather | solution.py:191
  522.7 122.7 %reduce-scatter.32.cloned.1.call-start = ((), (), s32[]{:S(2)}) async-start(), calls=%async_computation.30 | async-start | bytes 6488064 | tf_op jit(solution)/shard_map/reduce_scatter | solution.py:273
  532.1 169.2 %reduce-scatter.30.cloned.1.call-start = ((), (), s32[]{:S(2)}) async-start(), calls=%async_computation.29 | async-start | bytes 6488064 | tf_op jit(solution)/shard_map/reduce_scatter | solution.py:270
  540.9 222.8 %reduce-scatter.28.cloned.1.call-start = ((), (), s32[]{:S(2)}) async-start(), calls=%async_computation.28 | async-start | bytes 6488064 | tf_op jit(solution)/shard_map/reduce_scatter | solution.py:267
  549.9 251.2 %reduce-scatter.24.cloned.1.call-start = ((), (), s32[]{:S(2)}) async-start(), calls=%async_computation.26 | async-start | bytes 294912 | tf_op jit(solution)/shard_map/reduce_scatter | solution.py:258
  610.5 227.7 %reduce-scatter.22.cloned.1.call-start = ((), (), s32[]{:S(2)}) async-start(), calls=%async_computation.25 | async-start | bytes 294912 | tf_op jit(solution)/shard_map/reduce_scatter | solution.py:255
  613.6 269.4 %reduce-scatter.26.cloned.1.call-start = ((), (), s32[]{:S(2)}) async-start(), calls=%async_computation.27 | async-start | bytes 2359296 | tf_op jit(solution)/shard_map/reduce_scatter | solution.py:261
  618.9 308.5 %reduce-scatter.20.cloned.1.call-start = ((), (), s32[]{:S(2)}) async-start(), calls=%async_computation.24 | async-start | bytes 2359296 | tf_op jit(solution)/shard_map/reduce_scatter | solution.py:252
  627.8 354.1 %reduce-scatter.18.cloned.1.call-start = ((), (), s32[]{:S(2)}) async-start(), calls=%async_computation.23 | async-start | bytes 3276800 | tf_op jit(solution)/shard_map/reduce_scatter | solution.py:228
  633.8 402.3 %reduce-scatter.14.cloned.1.call-start = ((), (), s32[]{:S(2)}) async-start(), calls=%async_computation.19 | async-start | bytes 3276800 | tf_op jit(solution)/shard_map/reduce_scatter | solution.py:169
  647.7 334.2 %copy-start.34 = (f32[8,1,256]{2,1,0:T(1,128)S(1)}, f32[8,1,256]{2,1,0:T(1,128)}, u32[]{:S(2)}) copy-start(f32[8,1,256]{2,1,0:T(1,128)} %copy-done.33) | copy-start | bytes 24580
  647.7 334.2 %copy-start.40 = (f32[160]{0:T(256)S(1)}, f32[160]{0:T(256)}, u32[]{:S(2)}) copy-start(f32[160]{0:T(256)} %copy-done.39) | copy-start | bytes 1924
  703.7 279.9 %copy-start.38 = (bf16[2048]{0:T(1024)(128)(2,1)S(1)}, bf16[2048]{0:T(1024)(128)(2,1)}, u32[]{:S(2)}) copy-start(bf16[2048]{0:T(1024)(128)(2,1)} %get-tuple-element.51) | copy-start | bytes 12292
  703.7 332.4 %copy-start.4 = (bf16[160,2048]{1,0:T(8,128)(2,1)S(1)}, bf16[160,2048]{1,0:T(8,128)(2,1)}, u32[]{:S(2)}) copy-start(bf16[160,2048]{1,0:T(8,128)(2,1)} %reduce-scatter.12.cloned.1.call-done) | copy-start | bytes 1966084
  703.7 332.4 %copy-start.9 = (bf16[160,2048]{1,0:T(8,128)(2,1)S(1)}, bf16[160,2048]{1,0:T(8,128)(2,1)}, u32[]{:S(2)}) copy-start(bf16[160,2048]{1,0:T(8,128)(2,1)} %reduce-scatter.16.cloned.1.call-done) | copy-start | bytes 1966084
  703.7 332.4 %copy-start.10 = (bf16[160,2048]{1,0:T(8,128)(2,1)S(1)}, bf16[160,2048]{1,0:T(8,128)(2,1)}, u32[]{:S(2)}) copy-start(bf16[160,2048]{1,0:T(8,128)(2,1)} %param.31) | copy-start | bytes 1966084
  703.7 332.4 %copy-start.42 = (f32[160]{0:T(256)S(1)}, f32[160]{0:T(256)}, u32[]{:S(2)}) copy-start(f32[160]{0:T(256)} %copy-done.41) | copy-start | bytes 1924
  (42 other events, 234.0 us)
Sparse Core Ops, SparseCore 0:
  21.9 55.1 all-gather.11
  78.9 26.6 all-gather.13
  107.5 28.1 all-gather.15
  140.7 52.0 reduce-scatter.11
  194.6 42.9 all-gather.21
  239.6 54.7 all-gather.17
  296.4 42.0 all-gather.19
  340.1 54.8 all-gather.25
  396.8 43.1 all-gather.23
  465.0 52.0 reduce-scatter.15
  522.8 54.4 all-gather.27
  580.6 57.7 reduce-scatter.31
  642.3 59.0 reduce-scatter.29
  704.7 58.9 reduce-scatter.27
  767.4 33.5 reduce-scatter.23
  804.5 33.5 reduce-scatter.21
  841.7 41.2 reduce-scatter.25
  886.1 41.1 reduce-scatter.19
  929.7 52.0 reduce-scatter.17
  984.1 51.9 reduce-scatter.13
where the time goes:
time: 1060 us; the launch traced here: 1050 us
  waiting for transfers between devices  768 us (72%)
  matrix products  140 us (13%)
  blocking collectives  63.1 us (6%)
  other arithmetic  45.8 us (4%)
  between operations  16 us (2%)
  local copies, waits for them, and re-layouts  13.2 us (1%)
    reduce_scatter x1, waiting for transfers between devices, body(): lax.psum_scatter(grad_gate_local.astype(jnp.bfloat16), 'dp', scatter_dime...  60 us
    all_gather x1, waiting for transfers between devices, body(): lax.all_gather((unit_two * gain_two).astype(jnp.bfloat16), 'tensor', axis...  56.8 us
    reduce_scatter x1, waiting for transfers between devices, body(): lax.psum_scatter(grad_up_local.astype(jnp.bfloat16), 'dp', scatter_dimens...  53.7 us
    reduce_scatter x1, waiting for transfers between devices, body(): lax.psum_scatter((total + outer_t(d_value, full_value)).astype(jnp.bfloat...  52.7 us
    reduce_scatter x1, waiting for transfers between devices, body(): lax.psum_scatter((outer_t(d_gate, full_gate) + outer_t(d_up, full_up)).as...  52.2 us
    all_gather x1, waiting for transfers between devices, body(): cot_full = lax.all_gather(cotangent, 'tensor', axis=0, tiled=True)  47 us
    all_gather x1, waiting for transfers between devices, body(): lax.all_gather(w_down, 'dp', axis=1, tiled=True)  45 us
    reduce_scatter x1, waiting for transfers between devices, body(): lax.psum_scatter(grad_output_local.astype(jnp.bfloat16), 'dp', scatter_di...  43.4 us
  transfers between devices with their start and end apart: 20, of which 19 were waited for; matrix products, arithmetic and copies ran while one was open for 14% of the time, Pallas kernels for 0%

commit v1 on v0

v1 whole, which is shorter than its diff:
```python
import math

import jax
import jax.numpy as jnp
from jax import lax
from jax.sharding import PartitionSpec as P

HEAD_DIM = 64


EPS = 1e-05
ROPE_BASE = 10000.0
NEG_FILL = -1e30


def seq_layout(row_lengths, places):
    ends = jnp.cumsum(row_lengths)
    starts = ends - row_lengths
    segment = jnp.sum((places[:, None] >= ends[None, :]).astype(jnp.int32), axis=1)
    owner = segment[:, None] == jnp.arange(row_lengths.shape[0], dtype=jnp.int32)[None, :]
    begin = jnp.sum(jnp.where(owner, starts[None, :], 0), axis=1)
    return (segment, places - begin)


def rope_tables(position, head_dim):
    half = head_dim // 2
    freqs = ROPE_BASE ** (-(jnp.arange(half, dtype=jnp.float32) * 2.0 / head_dim))
    angles = position.astype(jnp.float32)[:, None] * freqs[None, :]
    cosine = jnp.cos(angles)
    sine = jnp.sin(angles)
    return (jnp.concatenate([cosine, cosine], 1), jnp.concatenate([sine, sine], 1))


def rotate(values, cosine, sine):
    half = values.shape[-1] // 2
    turned = jnp.concatenate([-values[..., half:], values[..., :half]], -1)
    return values * cosine[:, None, :] + turned * sine[:, None, :]


def unrotate(grads, cosine, sine):
    half = grads.shape[-1] // 2
    scaled = grads * sine[:, None, :]
    back = jnp.concatenate([scaled[..., half:], -scaled[..., :half]], -1)
    return grads * cosine[:, None, :] + back


def dot(left, right):
    return jnp.dot(left, right, preferred_element_type=jnp.float32)


def inner(left, right):
    return lax.dot_general(
        left, right, (((0,), (0,)), ((), ())), preferred_element_type=jnp.float32
    )


def outer_t(left, right):
    return lax.dot_general(
        left, right, (((1,), (1,)), ((), ())), preferred_element_type=jnp.float32
    )


def norm_back(d_normed, unit, inv, gain):
    scaled = d_normed * gain
    return inv * (scaled - unit * jnp.mean(scaled * unit, -1, keepdims=True))


def turn_by(block, step):
    count = lax.axis_size("tensor")
    return lax.ppermute(block, "tensor", [(i, (i + step) % count) for i in range(count)])


def spread(block):
    count = lax.axis_size("tensor")
    return [block] + [turn_by(block, step) for step in range(1, count)]


def collect(total):
    count = lax.axis_size("tensor")
    rows = total.shape[0] // count
    parts = [total[k * rows : (k + 1) * rows] for k in range(count)]
    return [parts[0]] + [turn_by(parts[k], -k) for k in range(1, count)]


def sum_of(parts):
    total = parts[0].astype(jnp.float32)
    for part in parts[1:]:
        total = total + part.astype(jnp.float32)
    return total


def body(
    tokens,
    lengths,
    attn_gain,
    w_query,
    w_key,
    w_value,
    w_output,
    ffn_gain,
    w_gate,
    w_up,
    w_down,
    cotangent,
):
    bf16 = jnp.bfloat16
    scale = 1.0 / math.sqrt(HEAD_DIM)
    count = lax.axis_size("tensor")
    local_rows = tokens.shape[0]
    group_rows = local_rows * count
    width = w_query.shape[1]
    kv_width = w_key.shape[1]
    hidden_units = w_gate.shape[1]
    kv_local = kv_width // HEAD_DIM
    q_local = width // HEAD_DIM
    group = q_local // kv_local

    token_parts = spread(tokens)
    attn_pack = lax.all_gather(
        jnp.concatenate([w_query, w_output.T, w_key, w_value], 1), "dp", axis=0, tiled=True
    )
    gains = lax.all_gather(
        jnp.stack([attn_gain, ffn_gain])[None], "dp", axis=0, tiled=True
    ).astype(jnp.float32)
    gain_one = gains[:, 0].reshape(-1)
    gain_two = gains[:, 1].reshape(-1)
    ffn_pack = lax.all_gather(
        jnp.concatenate([w_gate, w_up, w_down.T], 1), "dp", axis=0, tiled=True
    )
    cot_parts = lax.all_gather(cotangent, "tensor", axis=0, tiled=False)
    me = lax.axis_index("tensor")
    order = (me + count - jnp.arange(count, dtype=jnp.int32)) % count
    cot_full = jnp.take(cot_parts, order, axis=0).reshape(group_rows, -1)

    full_query = attn_pack[:, :width]
    full_output = attn_pack[:, width : 2 * width]
    full_kv = attn_pack[:, 2 * width :]
    full_gate = ffn_pack[:, :hidden_units]
    full_up = ffn_pack[:, hidden_units : 2 * hidden_units]
    full_down = ffn_pack[:, 2 * hidden_units :]

    places = (order[:, None] * local_rows + jnp.arange(local_rows, dtype=jnp.int32)[None]).reshape(
        -1
    )
    segment, position = seq_layout(lengths[0], places)
    cosine, sine = rope_tables(position, HEAD_DIM)
    allowed = (segment[:, None] == segment[None, :]) & (places[None, :] <= places[:, None])
    resid_full = jnp.concatenate(token_parts, 0).astype(jnp.float32)
    inv_full = lax.rsqrt(jnp.mean(resid_full * resid_full, -1, keepdims=True) + EPS)
    normed_one = (resid_full * inv_full * gain_one).astype(bf16)
    query = dot(normed_one, full_query).reshape(group_rows, q_local, HEAD_DIM)
    query = (
        rotate(query, cosine, sine).astype(bf16).reshape(group_rows, kv_local, group, HEAD_DIM)
    )
    key_value = dot(normed_one, full_kv)
    key = key_value[:, :kv_width].reshape(group_rows, kv_local, HEAD_DIM)
    key = rotate(key, cosine, sine).astype(bf16)
    value = key_value[:, kv_width:].astype(bf16).reshape(group_rows, kv_local, HEAD_DIM)
    scores = jnp.einsum("qcgd,kcd->cgqk", query, key, preferred_element_type=jnp.float32) * scale
    scores = jnp.where(allowed[None, None], scores, NEG_FILL)
    row_max = jnp.max(scores, -1, keepdims=True)
    raised = jnp.exp(scores - row_max)
    row_total = jnp.sum(raised, -1, keepdims=True)
    log_sums = row_max + jnp.log(row_total)
    prob = (raised / row_total).astype(bf16)
    attended = (
        jnp.einsum("cgqk,kcd->qcgd", prob, value, preferred_element_type=jnp.float32)
        .reshape(group_rows, width)
        .astype(bf16)
    )
    resid = tokens.astype(jnp.float32)
    hidden = resid + sum_of(collect(outer_t(attended, full_output).astype(bf16)))

    inv_two = lax.rsqrt(jnp.mean(hidden * hidden, -1, keepdims=True) + EPS)
    unit_two = hidden * inv_two
    normed_two = jnp.concatenate(spread((unit_two * gain_two).astype(bf16)), 0)
    gate = dot(normed_two, full_gate)
    up_part = dot(normed_two, full_up)
    sigma = jax.nn.sigmoid(gate)
    swish = gate * sigma
    activation = (swish * up_part).astype(bf16)
    d_act = dot(cot_full, full_down)
    d_gate = (d_act * up_part * (sigma * (1.0 + gate * (1.0 - sigma)))).astype(bf16)
    d_up = (d_act * swish).astype(bf16)
    d_normed_two = sum_of(
        collect((outer_t(d_gate, full_gate) + outer_t(d_up, full_up)).astype(bf16))
    )
    ffn_grads = lax.psum_scatter(
        jnp.concatenate(
            [
                inner(normed_two, d_gate).astype(bf16),
                inner(normed_two, d_up).astype(bf16),
                inner(cot_full, activation).astype(bf16),
            ],
            1,
        ),
        "dp",
        scatter_dimension=0,
        tiled=True,
    ).astype(jnp.float32)
    down_parts = outer_t(activation, full_down).astype(bf16).reshape(count, local_rows, -1)
    down_parts = jnp.take(down_parts, order, axis=0)
    block_out = (
        hidden
        + lax.psum_scatter(down_parts, "tensor", scatter_dimension=0, tiled=False).astype(
            jnp.float32
        )
    ).astype(bf16)

    gain_two_part = jnp.sum(d_normed_two * unit_two, 0)
    d_hidden = cotangent.astype(jnp.float32) + norm_back(d_normed_two, unit_two, inv_two, gain_two)
    d_hidden_full = jnp.concatenate(spread(d_hidden.astype(bf16)), 0)
    grad_output_local = inner(d_hidden_full, attended).astype(bf16)
    d_attended = (
        dot(d_hidden_full, full_output).astype(bf16).reshape(group_rows, kv_local, group, HEAD_DIM)
    )
    scores = jnp.einsum("qcgd,kcd->cgqk", query, key, preferred_element_type=jnp.float32) * scale
    scores = jnp.where(allowed[None, None], scores, NEG_FILL)
    prob = jnp.exp(scores - log_sums)
    d_prob = jnp.einsum("qcgd,kcd->cgqk", d_attended, value, preferred_element_type=jnp.float32)
    delta = jnp.sum(prob * d_prob, -1, keepdims=True)
    d_scores = (prob * (d_prob - delta)).astype(bf16)
    d_query = jnp.einsum("cgqk,kcd->qcgd", d_scores, key, preferred_element_type=jnp.float32)
    d_key = jnp.einsum("cgqk,qcgd->kcd", d_scores, query, preferred_element_type=jnp.float32)
    d_value = jnp.einsum(
        "cgqk,qcgd->kcd", prob.astype(bf16), d_attended, preferred_element_type=jnp.float32
    )
    d_query = d_query.reshape(group_rows, q_local, HEAD_DIM) * scale
    d_query = unrotate(d_query, cosine, sine).reshape(group_rows, width).astype(bf16)
    d_key = unrotate(d_key * scale, cosine, sine).reshape(group_rows, kv_width).astype(bf16)
    d_value = d_value.reshape(group_rows, kv_width).astype(bf16)
    d_kv = jnp.concatenate([d_key, d_value], 1)
    d_normed_full = outer_t(d_query, full_query) + outer_t(d_kv, full_kv)
    d_normed_one = sum_of(collect(d_normed_full.astype(bf16)))
    gain_one_part = jnp.sum(d_normed_full * (resid_full * inv_full), 0)
    inv_one = inv_full[:local_rows]
    grad_tokens = (
        d_hidden + norm_back(d_normed_one, resid * inv_one, inv_one, gain_one)
    ).astype(bf16)
    attn_grads = lax.psum_scatter(
        jnp.concatenate(
            [
                inner(normed_one, d_query).astype(bf16),
                grad_output_local,
                inner(normed_one, d_kv).astype(bf16),
            ],
            1,
        ),
        "dp",
        scatter_dimension=0,
        tiled=True,
    ).astype(jnp.float32)
    gain_grads = lax.psum(jnp.stack([gain_one_part, gain_two_part]), ("dp", "tensor"))
    own = attn_gain.shape[0]
    gain_grads = lax.dynamic_slice_in_dim(gain_grads, lax.axis_index("dp") * own, own, 1)
    return (
        block_out,
        grad_tokens,
        gain_grads[0],
        attn_grads[:, :width],
        attn_grads[:, 2 * width : 2 * width + kv_width],
        attn_grads[:, 2 * width + kv_width :],
        attn_grads[:, width : 2 * width].T,
        gain_grads[1],
        ffn_grads[:, :hidden_units],
        ffn_grads[:, hidden_units : 2 * hidden_units],
        ffn_grads[:, 2 * hidden_units :].T,
    )


def solution(mesh):
    return jax.shard_map(
        body,
        mesh=mesh,
        in_specs=(
            P(("dp", "tensor"), None),
            P("dp", None),
            P("dp"),
            P("dp", "tensor"),
            P("dp", "tensor"),
            P("dp", "tensor"),
            P("tensor", "dp"),
            P("dp"),
            P("dp", "tensor"),
            P("dp", "tensor"),
            P("tensor", "dp"),
            P(("dp", "tensor"), None),
        ),
        out_specs=(
            P(("dp", "tensor"), None),
            P(("dp", "tensor"), None),
            P("dp"),
            P("dp", "tensor"),
            P("dp", "tensor"),
            P("dp", "tensor"),
            P("tensor", "dp"),
            P("dp"),
            P("dp", "tensor"),
            P("dp", "tensor"),
            P("tensor", "dp"),
        ),
        check_vma=False,
    )
```

time: 1060 us -> 687 us (0.65)
  waiting for transfers between devices: 768 us -> 317 us
  starting transfers between devices: 1.53 us -> 64.2 us
  matrix products: 140 us -> 108 us
  local copies, waits for them, and re-layouts: 13.2 us -> 39.1 us
  blocking collectives: 63.1 us -> 84.4 us
    reduce_scatter x11 -> x3, waiting for transfers between devices: 445 us -> 50.5 us  [the longest x1 49.6 us: body(): lax.psum_scatter(jnp.concatenate([inner(normed_two, d_gate).astype(bf16),...]
    all_gather x9 -> x3, waiting for transfers between devices: 318 us -> 17 us  [the longest x1 17 us: body(): lax.all_gather(jnp.concatenate([w_gate, w_up, w_down.T], 1), 'dp', axis=0...]
    ppermute x0 -> x18, waiting for transfers between devices: none -> 248 us  [turn_by(): lax.ppermute(block, 'tensor', [(i, (i + step) % count) for i in range(cou...]
    psum x1, blocking collectives: 11.5 us -> 75.4 us  [body(): lax.psum(jnp.stack([gain_one_part, gain_two_part]), ('dp', 'tensor'))]
    ppermute x0 -> x18, starting transfers between devices: none -> 63.5 us  [turn_by(): lax.ppermute(block, 'tensor', [(i, (i + step) % count) for i in range(cou...]
    all_gather x4 -> x1, blocking collectives: 37.9 us -> 8.92 us  [body(): lax.all_gather(jnp.stack([attn_gain, ffn_gain])[None], 'dp', axis=0, tile...]
    concatenate x1 -> x4, other arithmetic: 0.03 us -> 14.8 us  [the longest x1 7.74 us: body(): jnp.concatenate([inner(normed_two, d_gate).astype(bf16), inner(normed_two...]
    dot_general x7 -> x6, matrix products: 38 us -> 23.4 us  [inner(): lax.dot_general(left, right, (((0,), (0,)), ((), ())), preferred_element_...]
  transfers between devices with their start and end apart: 20 -> 24, of which waited for: 19 -> 13; matrix products, arithmetic and copies ran while one was open for 14% -> 16% of each run, Pallas kernels for 0% -> 0%
where the time goes in v1:
time: 687 us; the launch traced here: 683 us
  waiting for transfers between devices  317 us (46%)
  matrix products  108 us (16%)
  blocking collectives  84.4 us (12%)
  starting transfers between devices  64.2 us (9%)
  other arithmetic  55.4 us (8%)
  local copies, waits for them, and re-layouts  39.1 us (6%)
  between operations  15.4 us (2%)
    ppermute x18, waiting for transfers between devices, turn_by(): lax.ppermute(block, 'tensor', [(i, (i + step) % count) for i in range(cou...  248 us
    psum x1, blocking collectives, body(): lax.psum(jnp.stack([gain_one_part, gain_two_part]), ('dp', 'tensor'))  75.4 us
    ppermute x18, starting transfers between devices, turn_by(): lax.ppermute(block, 'tensor', [(i, (i + step) % count) for i in range(cou...  63.5 us
    reduce_scatter x1, waiting for transfers between devices, body(): lax.psum_scatter(jnp.concatenate([inner(normed_two, d_gate).astype(bf16),...  49.6 us
    dot_general x6, matrix products, dot(): return jnp.dot(left, right, preferred_element_type=jnp.float32)  35.6 us
    dot_general x6, matrix products, outer_t(): lax.dot_general(left, right, (((1,), (1,)), ((), ())), preferred_element_...  32.5 us
    dot_general x6, matrix products, inner(): lax.dot_general(left, right, (((0,), (0,)), ((), ())), preferred_element_...  23.4 us
    unnamed x124, local copies, waits for them, and re-layouts  20 us
  transfers between devices with their start and end apart: 24, of which 13 were waited for; matrix products, arithmetic and copies ran while one was open for 16% of the time, Pallas kernels for 0%

profile of v1, /device:TPU:0, one launch (start us, length us, event | category | flops | bytes accessed | tf_op | source)
XLA Modules:
  0.0 683.1 jit_solution(13701645298987182851)
XLA Ops:
  14.5 5.1 collective-permute-start.2
  21.0 8.9 %all-gather.2 = bf16[8,2,256]{2,1,0:T(2,128)(2,1)S(1)} all-gather(bf16[1,2,256]{2,1,0:T(2,128)(2,1)S(1)} %maximum_bitcast_fusion), channel_id=2, replica_groups=mesh['dp'=8,'tensor'=4] {'dp'}, dimensions={0}, use_global_device_ids=true | all-gather | bytes 9216 | tf_op jit(solution)/shard_map/all_gather | solution.py:122
  34.8 67.6 %collective-permute-done.1 = bf16[160,2048]{1,0:T(8,128)(2,1)S(1)} collective-permute-done((bf16[160,2048]{1,0:T(8,128)(2,1)S(1)}, bf16[160,2048]{1,0:T(8,128)(2,1)S(1)}, u32[]{:S(2)}, u32[]{:S(2)}) %collective-permute-start.1) | collective-permute-done | bytes 655392 | tf_op jit(solution)/shard_map/ppermute | solution.py:70
  103.3 5.3 fusion.14
  127.4 3.7 convolution_convert_fusion.3
  133.9 4.3 collective-permute-start.5
  144.3 4.0 gather_fusion.1
  153.8 21.7 %collective-permute-done.4 = bf16[160,2048]{1,0:T(8,128)(2,1)S(1)} collective-permute-done((bf16[160,2048]{1,0:T(8,128)(2,1)}, bf16[160,2048]{1,0:T(8,128)(2,1)S(1)}, u32[]{:S(2)}, u32[]{:S(2)}) %collective-permute-start.4) | collective-permute-done | bytes 655392 | tf_op jit(solution)/shard_map/ppermute | solution.py:70
  178.8 20.4 %collective-permute-start.8 = (bf16[160,2048]{1,0:T(8,128)(2,1)S(1)}, bf16[160,2048]{1,0:T(8,128)(2,1)}, u32[]{:S(2)}, u32[]{:S(2)}) collective-permute-start(bf16[160,2048]{1,0:T(8,128)(2,1)S(1)} %multiply_convert_fusion.3), channel_id=1, source_target_pairs={{0,3},{1,0},{2,1},{3,2},{4,7},{5,4},{6,5},{7,6},{8,11},{9,8},{10,9... | collective-permute-start | bytes 1966088 | tf_op jit(solution)/shard_map/ppermute | solution.py:70
  199.8 17.0 %all-gather.9.cloned.1.call-done = bf16[2048,4224]{0,1:T(8,128)(2,1)} async-done(((bf16[256,4224]{0,1:T(8,128)(2,1)}), bf16[2048,4224]{0,1:T(8,128)(2,1)}) %all-gather.9.cloned.1.call-update) | async-done | bytes 17301520 | tf_op jit(solution)/shard_map/all_gather | solution.py:127
  216.8 7.5 %fusion.17 = f32[640,1408]{1,0:T(8,128)S(1)} fusion(bf16[640,2048]{1,0:T(8,128)(2,1)} %bitcast.170, bf16[2048,4224]{0,1:T(8,128)(2,1)} %all-gather.9.cloned.1.call-done), kind=kOutput, calls=%fused_computation.31 | convolution fusion | flops 3690987520 | bytes 11993088 | tf_op jit(solution)/shard_map/dot_general | solution.py:48
  224.3 26.8 %collective-permute-done.7 = bf16[160,2048]{1,0:T(8,128)(2,1)} collective-permute-done((bf16[160,2048]{1,0:T(8,128)(2,1)S(1)}, bf16[160,2048]{1,0:T(8,128)(2,1)}, u32[]{:S(2)}, u32[]{:S(2)}) %collective-permute-start.7) | collective-permute-done | bytes 655392 | tf_op jit(solution)/shard_map/ppermute | solution.py:70
  251.1 7.5 %fusion.23 = f32[640,1408]{1,0:T(8,128)S(1)} fusion(bf16[2048,4224]{0,1:T(8,128)(2,1)} %all-gather.9.cloned.1.call-done, bf16[160,2048]{1,0:T(8,128)(2,1)} %collective-permute-done.8, bf16[160,2048]{1,0:T(8,128)(2,1)} %collective-permute-done.7, bf16[160,2048]{1,0:T(8,128)(2,1)} %collective-permute-done.6, bf16[160,2048]{1,0:T(8,128)(2,1)S(1)} %multiply_convert_fusion.3), kind=kOutput, calls=%fused_computation.37 | convolution fusion | flops 3701473280 | bytes 11993088 | tf_op jit(solution)/shard_map/dot_general | solution.py:48
  258.6 10.7 %multiply_convert_fusion.1 = (bf16[640,1408]{1,0:T(8,128)(2,1)}, bf16[640,1408]{1,0:T(8,128)(2,1)}, bf16[640,1408]{1,0:T(8,128)(2,1)S(1)}) fusion(f32[640,1408]{1,0:T(8,128)S(1)} %fusion.17, f32[640,1408]{1,0:T(8,128)S(1)} %fusion.23, bf16[2048,4224]{0,1:T(8,128)(2,1)} %all-gather.9.cloned.1.call-done, bf16[160,2048]{1,0:T(8,128)(2,1)} %collective-permute-done.8, ...), kind=kOutput, calls=%fused_computation.45 | convolution fusion | flops 3714990080 | bytes 21004288 | tf_op jit(solution)/shard_map/dot_general | solution.py:48
  269.4 8.8 %fusion.30 = bf16[640,2048]{1,0:T(8,128)(2,1)} fusion(bf16[640,1408]{1,0:T(8,128)(2,1)S(1)} %get-tuple-element.53, bf16[2048,4224]{0,1:T(8,128)(2,1)} %all-gather.9.cloned.1.call-done), kind=kOutput, calls=%fused_computation.50 | convolution fusion | flops 3692298240 | bytes 10190848 | tf_op jit(solution)/shard_map/dot_general | solution.py:58
  278.1 4.1 gather_fusion
  286.1 6.9 %fusion.21 = f32[640,2048]{1,0:T(8,128)S(1)} fusion(bf16[640,1408]{1,0:T(8,128)(2,1)} %get-tuple-element.52, bf16[2048,4224]{0,1:T(8,128)(2,1)} %all-gather.9.cloned.1.call-done), kind=kOutput, calls=%fused_computation.35 | convolution fusion | flops 3690987520 | bytes 12812288 | tf_op jit(solution)/shard_map/dot_general | solution.py:58
  293.0 7.3 %add_convert_fusion = bf16[640,2048]{1,0:T(8,128)(2,1)S(1)} fusion(f32[640,2048]{1,0:T(8,128)S(1)} %fusion.21, bf16[640,1408]{1,0:T(8,128)(2,1)S(1)} %copy-done.53, bf16[2048,4224]{0,1:T(8,128)(2,1)} %all-gather.9.cloned.1.call-done), kind=kOutput, calls=%fused_computation.30 | convolution fusion | flops 3693608960 | bytes 15433728 | tf_op jit(solution)/shard_map/dot_general | solution.py:58
  305.3 28.6 %collective-permute-done.11 = bf16[160,2048]{1,0:T(8,128)(2,1)S(1)} collective-permute-done((bf16[160,2048]{1,0:T(8,128)(2,1)S(1)}, bf16[160,2048]{1,0:T(8,128)(2,1)S(1)}, u32[]{:S(2)}, u32[]{:S(2)}) %collective-permute-start.11) | collective-permute-done | bytes 655392 | tf_op jit(solution)/shard_map/ppermute | solution.py:70
  333.9 41.9 %collective-permute-done.10 = bf16[160,2048]{1,0:T(8,128)(2,1)S(1)} collective-permute-done((bf16[160,2048]{1,0:T(8,128)(2,1)S(1)}, bf16[160,2048]{1,0:T(8,128)(2,1)S(1)}, u32[]{:S(2)}, u32[]{:S(2)}) %collective-permute-start.10) | collective-permute-done | bytes 655392 | tf_op jit(solution)/shard_map/ppermute | solution.py:70
  378.6 4.3 fusion.90
  382.9 17.1 %collective-permute-start.14 = (bf16[160,2048]{1,0:T(8,128)(2,1)S(1)}, bf16[160,2048]{1,0:T(8,128)(2,1)S(1)}, u32[]{:S(2)}, u32[]{:S(2)}) collective-permute-start(bf16[160,2048]{1,0:T(8,128)(2,1)S(1)} %get-tuple-element.47), channel_id=1, source_target_pairs={{0,3},{1,0},{2,1},{3,2},{4,7},{5,4},{6,5},{7,6},{8,11},{9,8},{10,9... | collective-permute-start | bytes 1966088 | tf_op jit(solution)/shard_map/ppermute | solution.py:70
  400.6 14.5 %collective-permute-done.14 = bf16[160,2048]{1,0:T(8,128)(2,1)S(1)} collective-permute-done((bf16[160,2048]{1,0:T(8,128)(2,1)S(1)}, bf16[160,2048]{1,0:T(8,128)(2,1)S(1)}, u32[]{:S(2)}, u32[]{:S(2)}) %collective-permute-start.14) | collective-permute-done | bytes 655392 | tf_op jit(solution)/shard_map/ppermute | solution.py:70
  415.1 42.2 %collective-permute-done.13 = bf16[160,2048]{1,0:T(8,128)(2,1)S(1)} collective-permute-done((bf16[160,2048]{1,0:T(8,128)(2,1)S(1)}, bf16[160,2048]{1,0:T(8,128)(2,1)S(1)}, u32[]{:S(2)}, u32[]{:S(2)}) %collective-permute-start.13) | collective-permute-done | bytes 655392 | tf_op jit(solution)/shard_map/ppermute | solution.py:70
  460.9 6.1 fusion
  469.2 6.6 fusion.8
  489.7 6.8 convolution_convert_fusion.1
  496.5 7.2 %convolution_convert_fusion.2 = bf16[2048,1408]{0,1:T(8,128)(2,1)S(1)} fusion(bf16[640,1408]{1,0:T(8,128)(2,1)S(1)} %copy-done.54, bf16[160,2048]{1,0:T(8,128)(2,1)} %collective-permute-done.8, bf16[160,2048]{1,0:T(8,128)(2,1)} %collective-permute-done.7, bf16[160,2048]{1,0:T(8,128)(2,1)} %collective-permute-done.6, bf16[160,2048]{1,0:T(8,128)(2,1)S(1)} %copy-done.32), kind=kOutput, calls=%fused_computation.16 | convolution fusion | flops 3704356864 | bytes 10190848 | tf_op jit(solution)/shard_map/dot_general | solution.py:52
  503.8 5.0 convolution_convert_fusion
  508.8 7.7 %pad_maximum_fusion = bf16[2048,4224]{0,1:T(8,128)(2,1)} fusion(bf16[2048,1408]{0,1:T(8,128)(2,1)S(1)} %convolution_convert_fusion, bf16[2048,1408]{0,1:T(8,128)(2,1)S(1)} %convolution_convert_fusion.1, bf16[2048,1408]{0,1:T(8,128)(2,1)S(1)} %convolution_convert_fusion.2), kind=kLoop, calls=%fused_computation.2 | loop fusion | flops 51904512 | bytes 34603008 | tf_op jit(solution)/shard_map/concatenate | solution.py:189
  529.4 75.4 %psum.7 = f32[2,2048]{1,0:T(2,128)S(1)} all-reduce(f32[2,2048]{1,0:T(2,128)S(1)} %pad_maximum_fusion.15), channel_id=1, replica_groups=mesh['dp'=8,'tensor'=4] {'dp','tensor'}, use_global_device_ids=true, to_apply=%region_13.15 | all-reduce | flops 4096 | bytes 32768 | tf_op jit(solution)/shard_map/psum | solution.py:253
  615.7 49.6 %reduce-scatter.8.cloned.1.call-done = bf16[256,4224]{0,1:T(8,128)(2,1)} async-done(((bf16[2048,4224]{0,1:T(8,128)(2,1)}), bf16[256,4224]{0,1:T(8,128)(2,1)}) %reduce-scatter.8.cloned.1.call-update) | async-done | bytes 2162704 | tf_op jit(solution)/shard_map/reduce_scatter | solution.py:188
  (238 shorter events, 117.0 us)
Async XLA Ops:
  7.2 101.5 %all-gather.7.cloned.1.call-start = ((), (), s32[]{:S(2)}) async-start(), calls=%async_computation.3 | async-start | bytes 5308416 | tf_op jit(solution)/shard_map/all_gather | solution.py:119
  10.3 134.0 %all-gather.11.cloned.1.call-start = ((), (), s32[]{:S(2)}) async-start(), calls=%async_computation.8 | async-start | bytes 3276800 | tf_op jit(solution)/shard_map/all_gather | solution.py:130
  11.1 205.8 %all-gather.9.cloned.1.call-start = ((), (), s32[]{:S(2)}) async-start(), calls=%async_computation.4 | async-start | bytes 19464192 | tf_op jit(solution)/shard_map/all_gather | solution.py:127
  14.5 364.1 %reduce-scatter.4.cloned.1.call-start = ((), (), s32[]{:S(2)}) async-start(), calls=%async_computation.5 | async-start | bytes 3276800 | tf_op jit(solution)/shard_map/reduce_scatter | solution.py:205
  14.5 20.3 %collective-permute-start.2 = (bf16[160,2048]{1,0:T(8,128)(2,1)S(1)}, bf16[160,2048]{1,0:T(8,128)(2,1)S(1)}, u32[]{:S(2)}, u32[]{:S(2)}) collective-permute-start(bf16[160,2048]{1,0:T(8,128)(2,1)S(1)} %copy-done.1), channel_id=1, source_target_pairs={{0,3},{1,0},{2,1},{3,2},{4,7},{5,4},{6,5},{7,6},{8,11},{9,8},{10,9... | collective-permute-start | bytes 1966088 | tf_op jit(solution)/shard_map/ppermute | solution.py:70
  19.6 82.8 %collective-permute-start.1 = (bf16[160,2048]{1,0:T(8,128)(2,1)S(1)}, bf16[160,2048]{1,0:T(8,128)(2,1)S(1)}, u32[]{:S(2)}, u32[]{:S(2)}) collective-permute-start(bf16[160,2048]{1,0:T(8,128)(2,1)S(1)} %copy-done.1), channel_id=1, source_target_pairs={{0,2},{1,3},{2,0},{3,1},{4,6},{5,7},{6,4},{7,5},{8,10},{9,11},{10,... | collective-permute-start | bytes 1966088 | tf_op jit(solution)/shard_map/ppermute | solution.py:70
  19.6 82.8 %collective-permute-start = (bf16[160,2048]{1,0:T(8,128)(2,1)S(1)}, bf16[160,2048]{1,0:T(8,128)(2,1)S(1)}, u32[]{:S(2)}, u32[]{:S(2)}) collective-permute-start(bf16[160,2048]{1,0:T(8,128)(2,1)S(1)} %copy-done.1), channel_id=1, source_target_pairs={{0,1},{1,2},{2,3},{3,0},{4,5},{5,6},{6,7},{7,4},{8,9},{9,10},{10,1... | collective-permute-start | bytes 1966088 | tf_op jit(solution)/shard_map/ppermute | solution.py:70
  30.0 114.3 %copy-start.44 = (s32[1024]{0:T(1024)}, s32[1024]{0:T(1024)S(1)}, u32[]{:S(2)}) copy-start(s32[1024]{0:T(1024)S(1)} %pad_clamp_fusion) | copy-start | bytes 12292
  30.2 78.4 %copy-start.37 = (f32[8,1,256]{2,1,0:T(1,128)}, f32[8,1,256]{2,1,0:T(1,128)S(1)}, u32[]{:S(2)}) copy-start(f32[8,1,256]{2,1,0:T(1,128)S(1)} %get-tuple-element.86) | copy-start | bytes 24580
  30.6 81.0 %copy-start.22 = (f32[640,32]{0,1:T(8,128)}, f32[640,32]{0,1:T(8,128)S(1)}, u32[]{:S(2)}) copy-start(f32[640,32]{0,1:T(8,128)S(1)} %get-tuple-element.88) | copy-start | bytes 245764
  30.6 81.0 %copy-start.27 = (f32[640,32]{0,1:T(8,128)}, f32[640,32]{0,1:T(8,128)S(1)}, u32[]{:S(2)}) copy-start(f32[640,32]{0,1:T(8,128)S(1)} %get-tuple-element.87) | copy-start | bytes 245764
  133.9 19.8 %collective-permute-start.5 = (bf16[160,2048]{1,0:T(8,128)(2,1)}, bf16[160,2048]{1,0:T(8,128)(2,1)S(1)}, u32[]{:S(2)}, u32[]{:S(2)}) collective-permute-start(bf16[160,2048]{1,0:T(8,128)(2,1)} %get-tuple-element.63), channel_id=1, source_target_pairs={{0,1},{1,2},{2,3},{3,0},{4,5},{5,6},{6,7},{7,4},{8,9},{9,10},{10,1... | collective-permute-start | bytes 1966088 | tf_op jit(solution)/shard_map/ppermute | solution.py:70
  138.3 37.2 %collective-permute-start.4 = (bf16[160,2048]{1,0:T(8,128)(2,1)}, bf16[160,2048]{1,0:T(8,128)(2,1)S(1)}, u32[]{:S(2)}, u32[]{:S(2)}) collective-permute-start(bf16[160,2048]{1,0:T(8,128)(2,1)} %get-tuple-element.64), channel_id=1, source_target_pairs={{0,2},{1,3},{2,0},{3,1},{4,6},{5,7},{6,4},{7,5},{8,10},{9,11},{10,... | collective-permute-start | bytes 1966088 | tf_op jit(solution)/shard_map/ppermute | solution.py:70
  140.5 35.9 %collective-permute-start.3 = (bf16[160,2048]{1,0:T(8,128)(2,1)}, bf16[160,2048]{1,0:T(8,128)(2,1)}, u32[]{:S(2)}, u32[]{:S(2)}) collective-permute-start(bf16[160,2048]{1,0:T(8,128)(2,1)} %get-tuple-element.62), channel_id=1, source_target_pairs={{0,3},{1,0},{2,1},{3,2},{4,7},{5,4},{6,5},{7,6},{8,11},{9,8},{10,9... | collective-permute-start | bytes 1966088 | tf_op jit(solution)/shard_map/ppermute | solution.py:70
  178.8 79.8 %copy-start.31 = (bf16[160,2048]{1,0:T(8,128)(2,1)}, bf16[160,2048]{1,0:T(8,128)(2,1)S(1)}, u32[]{:S(2)}) copy-start(bf16[160,2048]{1,0:T(8,128)(2,1)S(1)} %multiply_convert_fusion.3) | copy-start | bytes 1966084
  178.8 45.5 %collective-permute-start.8 = (bf16[160,2048]{1,0:T(8,128)(2,1)S(1)}, bf16[160,2048]{1,0:T(8,128)(2,1)}, u32[]{:S(2)}, u32[]{:S(2)}) collective-permute-start(bf16[160,2048]{1,0:T(8,128)(2,1)S(1)} %multiply_convert_fusion.3), channel_id=1, source_target_pairs={{0,3},{1,0},{2,1},{3,2},{4,7},{5,4},{6,5},{7,6},{8,11},{9,8},{10,9... | collective-permute-start | bytes 1966088 | tf_op jit(solution)/shard_map/ppermute | solution.py:70
  199.2 51.9 %collective-permute-start.7 = (bf16[160,2048]{1,0:T(8,128)(2,1)S(1)}, bf16[160,2048]{1,0:T(8,128)(2,1)}, u32[]{:S(2)}, u32[]{:S(2)}) collective-permute-start(bf16[160,2048]{1,0:T(8,128)(2,1)S(1)} %multiply_convert_fusion.3), channel_id=1, source_target_pairs={{0,2},{1,3},{2,0},{3,1},{4,6},{5,7},{6,4},{7,5},{8,10},{9,11},{10,... | collective-permute-start | bytes 1966088 | tf_op jit(solution)/shard_map/ppermute | solution.py:70
  199.2 51.9 %collective-permute-start.6 = (bf16[160,2048]{1,0:T(8,128)(2,1)S(1)}, bf16[160,2048]{1,0:T(8,128)(2,1)}, u32[]{:S(2)}, u32[]{:S(2)}) collective-permute-start(bf16[160,2048]{1,0:T(8,128)(2,1)S(1)} %multiply_convert_fusion.3), channel_id=1, source_target_pairs={{0,1},{1,2},{2,3},{3,0},{4,5},{5,6},{6,7},{7,4},{8,9},{9,10},{10,1... | collective-permute-start | bytes 1966088 | tf_op jit(solution)/shard_map/ppermute | solution.py:70
  285.9 324.4 %reduce-scatter.6.cloned.1.call-start = ((), (), s32[]{:S(2)}) async-start(), calls=%async_computation.6 | async-start | bytes 5308416 | tf_op jit(solution)/shard_map/reduce_scatter | solution.py:240
  300.5 33.5 %collective-permute-start.11 = (bf16[160,2048]{1,0:T(8,128)(2,1)S(1)}, bf16[160,2048]{1,0:T(8,128)(2,1)S(1)}, u32[]{:S(2)}, u32[]{:S(2)}) collective-permute-start(bf16[160,2048]{1,0:T(8,128)(2,1)S(1)} %get-tuple-element.60), channel_id=1, source_target_pairs={{0,1},{1,2},{2,3},{3,0},{4,5},{5,6},{6,7},{7,4},{8,9},{9,10},{10,1... | collective-permute-start | bytes 1966088 | tf_op jit(solution)/shard_map/ppermute | solution.py:70
  300.5 75.3 %collective-permute-start.10 = (bf16[160,2048]{1,0:T(8,128)(2,1)S(1)}, bf16[160,2048]{1,0:T(8,128)(2,1)S(1)}, u32[]{:S(2)}, u32[]{:S(2)}) collective-permute-start(bf16[160,2048]{1,0:T(8,128)(2,1)S(1)} %get-tuple-element.61), channel_id=1, source_target_pairs={{0,2},{1,3},{2,0},{3,1},{4,6},{5,7},{6,4},{7,5},{8,10},{9,11},{10,... | collective-permute-start | bytes 1966088 | tf_op jit(solution)/shard_map/ppermute | solution.py:70
  302.4 73.5 %collective-permute-start.9 = (bf16[160,2048]{1,0:T(8,128)(2,1)S(1)}, bf16[160,2048]{1,0:T(8,128)(2,1)S(1)}, u32[]{:S(2)}, u32[]{:S(2)}) collective-permute-start(bf16[160,2048]{1,0:T(8,128)(2,1)S(1)} %get-tuple-element.59), channel_id=1, source_target_pairs={{0,3},{1,0},{2,1},{3,2},{4,7},{5,4},{6,5},{7,6},{8,11},{9,8},{10,9... | collective-permute-start | bytes 1966088 | tf_op jit(solution)/shard_map/ppermute | solution.py:70
  378.6 82.2 %slice-start = ((s8[13107200]{0:T(1024)(128)(4,1)}), s8[4194304]{0:T(1024)(128)(4,1)S(1)}, s32[]{:S(2)}) async-start(s8[13107200]{0:T(1024)(128)(4,1)} %bitcast.163), calls=%async_computation.9 | async-start | bytes 8388608
  382.9 32.2 %collective-permute-start.14 = (bf16[160,2048]{1,0:T(8,128)(2,1)S(1)}, bf16[160,2048]{1,0:T(8,128)(2,1)S(1)}, u32[]{:S(2)}, u32[]{:S(2)}) collective-permute-start(bf16[160,2048]{1,0:T(8,128)(2,1)S(1)} %get-tuple-element.47), channel_id=1, source_target_pairs={{0,3},{1,0},{2,1},{3,2},{4,7},{5,4},{6,5},{7,6},{8,11},{9,8},{10,9... | collective-permute-start | bytes 1966088 | tf_op jit(solution)/shard_map/ppermute | solution.py:70
  399.9 57.4 %collective-permute-start.13 = (bf16[160,2048]{1,0:T(8,128)(2,1)S(1)}, bf16[160,2048]{1,0:T(8,128)(2,1)S(1)}, u32[]{:S(2)}, u32[]{:S(2)}) collective-permute-start(bf16[160,2048]{1,0:T(8,128)(2,1)S(1)} %get-tuple-element.47), channel_id=1, source_target_pairs={{0,2},{1,3},{2,0},{3,1},{4,6},{5,7},{6,4},{7,5},{8,10},{9,11},{10,... | collective-permute-start | bytes 1966088 | tf_op jit(solution)/shard_map/ppermute | solution.py:70
  400.5 56.8 %collective-permute-start.12 = (bf16[160,2048]{1,0:T(8,128)(2,1)S(1)}, bf16[160,2048]{1,0:T(8,128)(2,1)S(1)}, u32[]{:S(2)}, u32[]{:S(2)}) collective-permute-start(bf16[160,2048]{1,0:T(8,128)(2,1)S(1)} %get-tuple-element.47), channel_id=1, source_target_pairs={{0,1},{1,2},{2,3},{3,0},{4,5},{5,6},{6,7},{7,4},{8,9},{9,10},{10,1... | collective-permute-start | bytes 1966088 | tf_op jit(solution)/shard_map/ppermute | solution.py:70
  488.7 176.7 %reduce-scatter.8.cloned.1.call-start = ((), (), s32[]{:S(2)}) async-start(), calls=%async_computation.7 | async-start | bytes 19464192 | tf_op jit(solution)/shard_map/reduce_scatter | solution.py:188
  522.4 83.1 %copy-start.38 = (f32[8,1,256]{2,1,0:T(1,128)S(1)}, f32[8,1,256]{2,1,0:T(1,128)}, u32[]{:S(2)}) copy-start(f32[8,1,256]{2,1,0:T(1,128)} %copy-done.37) | copy-start | bytes 24580
  525.3 82.1 %copy-start.8 = (f32[160,2048]{1,0:T(8,128)S(1)}, f32[160,2048]{1,0:T(8,128)}, u32[]{:S(2)}) copy-start(f32[160,2048]{1,0:T(8,128)} %get-tuple-element.48) | copy-start | bytes 3932164
  525.3 80.2 %collective-permute-start.17 = (bf16[160,2048]{1,0:T(8,128)(2,1)}, bf16[160,2048]{1,0:T(8,128)(2,1)S(1)}, u32[]{:S(2)}, u32[]{:S(2)}) collective-permute-start(bf16[160,2048]{1,0:T(8,128)(2,1)} %get-tuple-element.57), channel_id=1, source_target_pairs={{0,1},{1,2},{2,3},{3,0},{4,5},{5,6},{6,7},{7,4},{8,9},{9,10},{10,1... | collective-permute-start | bytes 1966088 | tf_op jit(solution)/shard_map/ppermute | solution.py:70
  525.3 80.2 %collective-permute-start.16 = (bf16[160,2048]{1,0:T(8,128)(2,1)}, bf16[160,2048]{1,0:T(8,128)(2,1)S(1)}, u32[]{:S(2)}, u32[]{:S(2)}) collective-permute-start(bf16[160,2048]{1,0:T(8,128)(2,1)} %get-tuple-element.58), channel_id=1, source_target_pairs={{0,2},{1,3},{2,0},{3,1},{4,6},{5,7},{6,4},{7,5},{8,10},{9,11},{10,... | collective-permute-start | bytes 1966088 | tf_op jit(solution)/shard_map/ppermute | solution.py:70
  526.5 79.0 %collective-permute-start.15 = (bf16[160,2048]{1,0:T(8,128)(2,1)}, bf16[160,2048]{1,0:T(8,128)(2,1)}, u32[]{:S(2)}, u32[]{:S(2)}) collective-permute-start(bf16[160,2048]{1,0:T(8,128)(2,1)} %get-tuple-element.56), channel_id=1, source_target_pairs={{0,3},{1,0},{2,1},{3,2},{4,7},{5,4},{6,5},{7,6},{8,11},{9,8},{10,9... | collective-permute-start | bytes 1966088 | tf_op jit(solution)/shard_map/ppermute | solution.py:70
  (51 other events, 615.8 us)
Sparse Core Ops, SparseCore 0:
  10.5 42.4 all-gather.6
  54.5 64.0 all-gather.10
  120.6 96.2 all-gather.8
  286.0 92.5 reduce-scatter.3
  488.8 53.2 reduce-scatter.5
  546.1 119.2 reduce-scatter.7

commit v2 on v1

v2 whole, which is shorter than its diff:
```python
import functools
import math

import jax
import jax.numpy as jnp
from jax import lax
from jax.experimental import pallas as pl
from jax.experimental.pallas import tpu as pltpu
from jax.sharding import PartitionSpec as P

HEAD_DIM = 64
EPS = 1e-05
ROPE_BASE = 10000.0
NEG_FILL = -1e30
MIB = 1024 * 1024


def seq_layout(row_lengths, places):
    ends = jnp.cumsum(row_lengths)
    starts = ends - row_lengths
    segment = jnp.sum((places[:, None] >= ends[None, :]).astype(jnp.int32), axis=1)
    owner = segment[:, None] == jnp.arange(row_lengths.shape[0], dtype=jnp.int32)[None, :]
    begin = jnp.sum(jnp.where(owner, starts[None, :], 0), axis=1)
    return (segment, places - begin)


def rope_tables(position):
    half = HEAD_DIM // 2
    freqs = ROPE_BASE ** (-(jnp.arange(half, dtype=jnp.float32) * 2.0 / HEAD_DIM))
    angles = freqs[:, None] * position.astype(jnp.float32)[None, :]
    return (jnp.cos(angles), jnp.sin(angles))


def dot(left, right):
    return jnp.dot(left, right, preferred_element_type=jnp.float32)


def inner(left, right):
    return lax.dot_general(
        left, right, (((0,), (0,)), ((), ())), preferred_element_type=jnp.float32
    )


def outer_t(left, right):
    return lax.dot_general(
        left, right, (((1,), (1,)), ((), ())), preferred_element_type=jnp.float32
    )


def norm_back(d_normed, unit, inv, gain):
    scaled = d_normed * gain
    return inv * (scaled - unit * jnp.mean(scaled * unit, -1, keepdims=True))


def swap(block, *pairs):
    return lax.ppermute(block, "tensor", [p for i, j in pairs for p in ((i, j), (j, i))])


def outward(block):
    return lax.ppermute(block, "tensor", [(1, 0), (2, 3)])


def inward(block):
    return lax.ppermute(block, "tensor", [(0, 1), (3, 2)])


def spread(block):
    two = swap(block, (0, 2), (1, 3))
    one = swap(block, (0, 1), (2, 3))
    three = swap(block, (1, 2))
    return [one, two, three]


def whole(block, one, two, three, far):
    me = lax.axis_index("tensor")
    return jnp.concatenate([block, one, two, jnp.where((me == 1) | (me == 2), three, far)], 0)


def split(total):
    count = lax.axis_size("tensor")
    rows = total.shape[0] // count
    return [total[k * rows : (k + 1) * rows] for k in range(count)]


def add(left, right):
    return (left.astype(jnp.float32) + right.astype(jnp.float32)).astype(left.dtype)


def collect(total, *others):
    parts = split(total)
    far = inward(parts[3])
    far, parts, *others = lax.optimization_barrier((far, parts, *others))
    one = swap(parts[1], (0, 1), (2, 3))
    three = swap(parts[3], (1, 2))
    two = swap(add(parts[2], far), (0, 2), (1, 3))
    return ([parts[0], one, two, three], *others)


def after(value, *others):
    return lax.optimization_barrier((value, *others))[0]


def grads_kernel(count, *refs):
    lefts, rights, out = refs[:count], refs[count:-1], refs[-1]
    at = 0
    for left, right in zip(lefts, rights):
        width = right.shape[1]
        out[:, at : at + width] = inner(left[...], right[...]).astype(out.dtype)
        at += width
    for extra in rights[count:]:
        width = extra.shape[1]
        out[:, at : at + width] = extra[...]
        at += width


def grads_of(pairs, extras=()):
    rows, depth = pairs[0][0].shape
    block = min(256, depth)
    width = sum(right.shape[1] for _, right in pairs) + sum(e.shape[1] for e in extras)
    return pl.pallas_call(
        lambda *refs: grads_kernel(len(pairs), *refs),
        grid=(depth // block,),
        out_shape=jax.ShapeDtypeStruct((depth, width), jnp.bfloat16),
        in_specs=[pl.BlockSpec((rows, block), lambda i: (0, i)) for _ in pairs]
        + [pl.BlockSpec(right.shape, lambda i: (0, 0)) for _, right in pairs]
        + [pl.BlockSpec((block, e.shape[1]), lambda i: (i, 0)) for e in extras],
        out_specs=pl.BlockSpec((block, width), lambda i: (i, 0)),
        cost_estimate=pl.CostEstimate(
            flops=2 * rows * depth * width,
            bytes_accessed=2 * (depth * width + rows * width + 2 * rows * depth),
            transcendentals=0,
        ),
        compiler_params=pltpu.CompilerParams(vmem_limit_bytes=40 * MIB),
    )(*[left for left, _ in pairs], *[right for _, right in pairs], *extras)


def sum_of(parts):
    total = parts[0].astype(jnp.float32)
    for part in parts[1:]:
        total = total + part.astype(jnp.float32)
    return total


def turn(block, cosine, sine):
    half = HEAD_DIM // 2
    first, second = block[:half], block[half:]
    return jnp.concatenate([first * cosine - second * sine, second * cosine + first * sine], 0)

def mask_bias(row_ref, col_ref, bias):
    allowed = (col_ref[:, 0:1] == row_ref[0:1, :]) & (col_ref[:, 1:2] <= row_ref[1:2, :])
    bias[...] = jnp.where(allowed, 0.0, NEG_FILL)

def attend_kernel(q_width, kv_width, x_ref, gain_ref, pack_ref, cos_ref, sin_ref, row_ref, col_ref,
                  out_ref, normed_ref, heads_ref, attended_ref, sums_ref, bias):
    bf16 = jnp.bfloat16
    scale = 1.0 / math.sqrt(HEAD_DIM)
    q_heads, kv_heads = q_width // HEAD_DIM, kv_width // HEAD_DIM
    qkv = q_width + 2 * kv_width
    x = x_ref[...].astype(jnp.float32)
    inv = lax.rsqrt(jnp.mean(x * x, -1, keepdims=True) + EPS)
    normed_ref[...] = (x * inv * gain_ref[...]).astype(bf16)
    mask_bias(row_ref, col_ref, bias)
    cosine, sine = cos_ref[...], sin_ref[...]
    heads = dot(normed_ref[...], pack_ref[:, :qkv]).T
    for h in range(q_heads + kv_heads):
        at = h * HEAD_DIM
        turned = turn(heads[at : at + HEAD_DIM], cosine, sine).astype(bf16)
        heads_ref[at : at + HEAD_DIM] = turned * bf16(scale) if h < q_heads else turned
    heads_ref[q_width + kv_width :] = heads[q_width + kv_width :].astype(bf16)
    parts = []
    for h in range(q_heads):
        c = h * kv_heads // q_heads
        at = q_width + c * HEAD_DIM
        key = heads_ref[at : at + HEAD_DIM].T
        value_t = heads_ref[at + kv_width : at + kv_width + HEAD_DIM]
        scores = dot(key, heads_ref[h * HEAD_DIM : (h + 1) * HEAD_DIM]) + bias[...]
        top = jnp.max(scores, 0, keepdims=True)
        raised = jnp.exp(scores - top)
        total = jnp.sum(raised, 0, keepdims=True)
        sums_ref[h : h + 1] = top + jnp.log(total)
        parts.append(dot(value_t, raised.astype(bf16)) / total)
    attended_ref[...] = jnp.concatenate(parts, 0).T.astype(bf16)
    out_ref[...] = outer_t(attended_ref[...], pack_ref[:, qkv:]).astype(bf16)

def attend(x, gain, pack, cosine, sine, row, col, q_width, kv_width):
    rows, depth = x.shape
    bf16 = jnp.bfloat16
    qkv = q_width + 2 * kv_width
    return pl.pallas_call(
        functools.partial(attend_kernel, q_width, kv_width),
        out_shape=(
            jax.ShapeDtypeStruct((rows, depth), bf16),
            jax.ShapeDtypeStruct((rows, depth), bf16),
            jax.ShapeDtypeStruct((qkv, rows), bf16),
            jax.ShapeDtypeStruct((rows, q_width), bf16),
            jax.ShapeDtypeStruct((q_width // HEAD_DIM, rows), jnp.float32),
        ),
        scratch_shapes=[pltpu.VMEM((rows, rows), jnp.float32)],
        cost_estimate=pl.CostEstimate(
            flops=2 * rows * depth * (qkv + q_width) + 4 * rows * rows * q_width,
            bytes_accessed=2 * (3 * rows * depth + depth * (qkv + q_width)),
            transcendentals=rows * rows * q_width // HEAD_DIM,
        ),
        compiler_params=pltpu.CompilerParams(vmem_limit_bytes=48 * MIB),
    )(x, gain, pack, cosine, sine, row, col)

def attend_back_kernel(q_width, kv_width, g_ref, x_ref, gain_ref, pack_ref, cos_ref, sin_ref, row_ref, col_ref,
                       heads_ref, sums_ref, out_ref, d_qkv_ref, gain_part_ref, bias, d_att_t, d_heads_t):
    bf16 = jnp.bfloat16
    scale = 1.0 / math.sqrt(HEAD_DIM)
    q_heads, kv_heads = q_width // HEAD_DIM, kv_width // HEAD_DIM
    qkv = q_width + 2 * kv_width
    mask_bias(row_ref, col_ref, bias)
    d_att_t[...] = dot(g_ref[...], pack_ref[:, qkv:]).T.astype(bf16)
    cosine, sine = cos_ref[...], sin_ref[...]
    for c in range(kv_heads):
        at = q_width + c * HEAD_DIM
        key_t = heads_ref[at : at + HEAD_DIM]
        key = key_t.T
        value = heads_ref[at + kv_width : at + kv_width + HEAD_DIM].T
        d_key = d_value = 0.0
        for h in range(c * q_heads // kv_heads, (c + 1) * q_heads // kv_heads):
            query_t = heads_ref[h * HEAD_DIM : (h + 1) * HEAD_DIM]
            d_out_t = d_att_t[h * HEAD_DIM : (h + 1) * HEAD_DIM]
            prob = jnp.exp(dot(key, query_t) + bias[...] - sums_ref[h : h + 1])
            d_prob = dot(value, d_out_t)
            delta = jnp.sum(prob * d_prob, 0, keepdims=True)
            d_scores = (prob * (d_prob - delta)).astype(bf16)
            d_value = d_value + outer_t(prob.astype(bf16), d_out_t)
            d_key = d_key + outer_t(d_scores, query_t)
            d_query = dot(key_t, d_scores) * scale
            d_heads_t[h * HEAD_DIM : (h + 1) * HEAD_DIM] = turn(d_query, cosine, -sine)
        d_heads_t[at : at + HEAD_DIM] = turn(d_key.T, cosine, -sine)
        d_heads_t[at + kv_width : at + kv_width + HEAD_DIM] = d_value.T
    d_qkv_ref[...] = d_heads_t[...].T.astype(bf16)
    d_normed = outer_t(d_qkv_ref[...], pack_ref[:, :qkv])
    out_ref[...] = d_normed.astype(bf16)
    x = x_ref[...].astype(jnp.float32)
    inv = lax.rsqrt(jnp.mean(x * x, -1, keepdims=True) + EPS)
    gain_part_ref[...] = jnp.sum(d_normed * (x * inv), 0, keepdims=True)

def attend_back(g, x, gain, pack, cosine, sine, row, col, heads, sums, q_width, kv_width):
    rows, depth = x.shape
    bf16 = jnp.bfloat16
    qkv = q_width + 2 * kv_width
    return pl.pallas_call(
        functools.partial(attend_back_kernel, q_width, kv_width),
        out_shape=(
            jax.ShapeDtypeStruct((rows, depth), bf16),
            jax.ShapeDtypeStruct((rows, qkv), bf16),
            jax.ShapeDtypeStruct((1, depth), jnp.float32),
        ),
        scratch_shapes=[
            pltpu.VMEM((rows, rows), jnp.float32),
            pltpu.VMEM((q_width, rows), bf16),
            pltpu.VMEM((qkv, rows), jnp.float32),
        ],
        cost_estimate=pl.CostEstimate(
            flops=2 * rows * depth * (qkv + q_width) + 10 * rows * rows * q_width,
            bytes_accessed=2 * (3 * rows * depth + depth * (qkv + q_width)),
            transcendentals=rows * rows * q_width // HEAD_DIM,
        ),
        compiler_params=pltpu.CompilerParams(vmem_limit_bytes=56 * MIB),
    )(g, x, gain, pack, cosine, sine, row, col, heads, sums)


def body(
    tokens,
    lengths,
    attn_gain,
    w_query,
    w_key,
    w_value,
    w_output,
    ffn_gain,
    w_gate,
    w_up,
    w_down,
    cotangent,
):
    bf16 = jnp.bfloat16
    count = lax.axis_size("tensor")
    local_rows = tokens.shape[0]
    width = w_query.shape[1]
    kv_width = w_key.shape[1]
    hidden_units = w_gate.shape[1]

    token_parts = spread(tokens)
    attn_pack = lax.all_gather(
        jnp.concatenate([w_query, w_key, w_value, w_output.T], 1), "dp", axis=0, tiled=True
    )
    gains = lax.all_gather(
        jnp.stack([attn_gain, ffn_gain])[None], "dp", axis=0, tiled=True
    ).astype(jnp.float32)
    gain_one = gains[:, 0].reshape(1, -1)
    gain_two = gains[:, 1].reshape(1, -1)
    ffn_pack = lax.all_gather(
        jnp.concatenate([w_gate, w_up, w_down.T], 1),
        "dp",
        axis=0,
        tiled=True,
    )
    token_parts.append(outward(token_parts[1]))
    cot_own, token_parts = lax.optimization_barrier((cotangent, token_parts))
    cot_parts = spread(cot_own)
    full_gate_up = ffn_pack[:, : 2 * hidden_units]
    full_down = ffn_pack[:, 2 * hidden_units :]

    order = lax.axis_index("tensor") ^ jnp.arange(count, dtype=jnp.int32)
    places = (order[:, None] * local_rows + jnp.arange(local_rows, dtype=jnp.int32)[None]).reshape(
        -1
    )
    segment, position = seq_layout(lengths[0], places)
    cosine, sine = rope_tables(position)
    as_row = jnp.stack([segment, places])
    as_column = jnp.stack([segment, places], 1)
    token_rows = whole(tokens, *token_parts)
    out_total, normed_one, heads, attended, log_sums = attend(
        token_rows, gain_one, attn_pack, cosine, sine, as_row, as_column, width, kv_width
    )
    out_parts, cot_parts = collect(out_total, cot_parts)
    cot_parts.append(outward(cot_parts[1]))
    out_parts, cot_parts = lax.optimization_barrier((out_parts, cot_parts))
    resid = tokens.astype(jnp.float32)
    hidden = resid + sum_of(out_parts)

    inv_two = lax.rsqrt(jnp.mean(hidden * hidden, -1, keepdims=True) + EPS)
    unit_two = hidden * inv_two
    own_two = (unit_two * gain_two).astype(bf16)
    two_rows = spread(own_two)
    two_rows.append(outward(two_rows[1]))
    normed_two = whole(own_two, *two_rows)
    gate_up = dot(normed_two, full_gate_up)
    gate = gate_up[:, :hidden_units]
    up_part = gate_up[:, hidden_units:]
    sigma = jax.nn.sigmoid(gate)
    swish = gate * sigma
    activation = (swish * up_part).astype(bf16)
    cot_full = whole(cotangent, *cot_parts)
    d_act = dot(cot_full, full_down)
    d_gate = (d_act * up_part * (sigma * (1.0 + gate * (1.0 - sigma)))).astype(bf16)
    d_up = (d_act * swish).astype(bf16)
    d_gate_up = jnp.concatenate([d_gate, d_up], 1)
    two_total = outer_t(d_gate_up, full_gate_up).astype(bf16)
    two_parts, activation, d_gate_up = collect(two_total, activation, d_gate_up)
    ffn_local = grads_of([(normed_two, d_gate_up), (cot_full, activation)])
    down_total = outer_t(activation, full_down).astype(bf16)
    two_parts, ffn_local, down_total = lax.optimization_barrier((two_parts, ffn_local, down_total))
    ffn_grads = lax.psum_scatter(ffn_local, "dp", scatter_dimension=0, tiled=True)
    d_normed_two = sum_of(two_parts)

    gain_two_part = jnp.sum(d_normed_two * unit_two, 0)
    d_hidden = cotangent.astype(jnp.float32) + norm_back(d_normed_two, unit_two, inv_two, gain_two)
    d_hidden_own = d_hidden.astype(bf16)
    back_rows = spread(d_hidden_own)
    down_parts, back_rows = collect(down_total, back_rows)
    back_rows.append(outward(back_rows[1]))
    d_hidden_full = whole(d_hidden_own, *back_rows)
    one_total, d_qkv, gain_one_part = attend_back(
        d_hidden_full,
        token_rows,
        gain_one,
        attn_pack,
        cosine,
        sine,
        as_row,
        as_column,
        heads,
        log_sums,
        width,
        kv_width,
    )
    one_total, down_parts = lax.optimization_barrier((one_total, down_parts))
    one_parts, d_qkv, gain_one_part = collect(one_total, d_qkv, gain_one_part)
    gain_parts = jnp.stack([gain_one_part[0], gain_two_part])
    gain_parts = sum_of(
        [gain_parts]
        + [
            lax.ppermute(gain_parts, "tensor", [(i, (i + k) % count) for i in range(count)])
            for k in range(1, count)
        ]
    )
    attn_local = grads_of(
        [(normed_one, d_qkv), (d_hidden_full, attended)],
        [jnp.pad(gain_parts.T.astype(bf16), ((0, 0), (0, 126)))],
    )
    attn_local, ffn_grads, one_parts[1:2] = lax.optimization_barrier(
        (attn_local, ffn_grads, one_parts[1:2])
    )
    attn_grads = lax.psum_scatter(attn_local, "dp", scatter_dimension=0, tiled=True).astype(
        jnp.float32
    )
    ffn_grads = ffn_grads.astype(jnp.float32)
    block_out = (hidden + sum_of(down_parts)).astype(bf16)
    inv_one = lax.rsqrt(jnp.mean(resid * resid, -1, keepdims=True) + EPS)
    grad_tokens = (
        d_hidden + norm_back(sum_of(one_parts), resid * inv_one, inv_one, gain_one)
    ).astype(bf16)
    at_output = width + 2 * kv_width
    return (
        block_out,
        grad_tokens,
        attn_grads[:, at_output + width],
        attn_grads[:, :width],
        attn_grads[:, width : width + kv_width],
        attn_grads[:, width + kv_width : at_output],
        attn_grads[:, at_output : at_output + width].T,
        attn_grads[:, at_output + width + 1],
        ffn_grads[:, :hidden_units],
        ffn_grads[:, hidden_units : 2 * hidden_units],
        ffn_grads[:, 2 * hidden_units :].T,
    )


def solution(mesh):
    return jax.shard_map(
        body,
        mesh=mesh,
        in_specs=(
            P(("dp", "tensor"), None),
            P("dp", None),
            P("dp"),
            P("dp", "tensor"),
            P("dp", "tensor"),
            P("dp", "tensor"),
            P("tensor", "dp"),
            P("dp"),
            P("dp", "tensor"),
            P("dp", "tensor"),
            P("tensor", "dp"),
            P(("dp", "tensor"), None),
        ),
        out_specs=(
            P(("dp", "tensor"), None),
            P(("dp", "tensor"), None),
            P("dp"),
            P("dp", "tensor"),
            P("dp", "tensor"),
            P("dp", "tensor"),
            P("tensor", "dp"),
            P("dp"),
            P("dp", "tensor"),
            P("dp", "tensor"),
            P("tensor", "dp"),
        ),
        check_vma=False,
    )
```

time: 687 us -> 517 us (0.75)
  blocking collectives: 84.4 us -> 8.91 us
  matrix products: 108 us -> 44.7 us
  waiting for transfers between devices: 317 us -> 257 us
  Pallas kernels: 0 us -> 56.8 us
  other arithmetic: 55.4 us -> 29.9 us
    psum x1 -> x0, blocking collectives: 75.4 us -> none  [body(): lax.psum(jnp.stack([gain_one_part, gain_two_part]), ('dp', 'tensor'))]
    pallas_call x0 -> x4, Pallas kernels: none -> 56.8 us  [the longest x2 24 us: grads_of(): pl.pallas_call(lambda *refs: grads_kernel(len(pairs), *refs), grid=(depth...]
    dot_general x12 -> x0, matrix products: 39.8 us -> none  [the longest x6 23.4 us: inner(): lax.dot_general(left, right, (((0,), (0,)), ((), ())), preferred_element_...]
    reduce_scatter x3 -> x2, waiting for transfers between devices: 50.5 us -> 21.1 us  [the longest x1 21.1 us: body(): lax.psum_scatter(attn_local, 'dp', scatter_dimension=0, tiled=True)]
    all_gather x1, waiting for transfers between devices: 17 us -> 0.01 us  [body(): lax.all_gather(jnp.concatenate([w_gate, w_up, w_down.T], 1), 'dp', axis=0...]
    ppermute x18 -> x35, waiting for transfers between devices: 248 us -> 236 us  [the longest x24 140 us: swap(): lax.ppermute(block, 'tensor', [p for i, j in pairs for p in ((i, j), (j,...]
    dot_general x6 -> x2, matrix products: 32.5 us -> 20.2 us  [outer_t(): lax.dot_general(left, right, (((1,), (1,)), ((), ())), preferred_element_...]
    dot_general x6 -> x2, matrix products: 35.6 us -> 24.5 us  [dot(): return jnp.dot(left, right, preferred_element_type=jnp.float32)]
  transfers between devices with their start and end apart: 24 -> 39, of which waited for: 13 -> 16; matrix products, arithmetic and copies ran while one was open for 16% -> 10% of each run, Pallas kernels for 0% -> 11%
where the time goes in v2:
time: 517 us; the launch traced here: 516 us
  waiting for transfers between devices  257 us (50%)
  starting transfers between devices  68.4 us (13%)
  Pallas kernels  56.8 us (11%)
  matrix products  44.7 us (9%)
  local copies, waits for them, and re-layouts  35.7 us (7%)
  other arithmetic  29.9 us (6%)
  between operations  15.1 us (3%)
  blocking collectives  8.91 us (2%)
    ppermute x24, waiting for transfers between devices, swap(): lax.ppermute(block, 'tensor', [p for i, j in pairs for p in ((i, j), (j,...  140 us
    ppermute x4, waiting for transfers between devices, outward(): return lax.ppermute(block, 'tensor', [(1, 0), (2, 3)])  67.7 us
    ppermute x24, starting transfers between devices, swap(): lax.ppermute(block, 'tensor', [p for i, j in pairs for p in ((i, j), (j,...  48 us
    dot_general x2, matrix products, dot(): return jnp.dot(left, right, preferred_element_type=jnp.float32)  24.5 us
    pallas_call x2, Pallas kernels, grads_of(): pl.pallas_call(lambda *refs: grads_kernel(len(pairs), *refs), grid=(depth...  24 us
    ppermute x4, waiting for transfers between devices, inward(): return lax.ppermute(block, 'tensor', [(0, 1), (3, 2)])  22.7 us
    reduce_scatter x1, waiting for transfers between devices, body(): lax.psum_scatter(attn_local, 'dp', scatter_dimension=0, tiled=True)  21.1 us
    dot_general x2, matrix products, outer_t(): lax.dot_general(left, right, (((1,), (1,)), ((), ())), preferred_element_...  20.2 us
  transfers between devices with their start and end apart: 39, of which 16 were waited for; matrix products, arithmetic and copies ran while one was open for 10% of the time, Pallas kernels for 11%

profile of v2, /device:TPU:0, one launch (start us, length us, event | category | flops | bytes accessed | tf_op | source)
XLA Modules:
  0.0 516.4 jit_solution(12728061704911382484)
XLA Ops:
  14.4 4.1 collective-permute-start.1
  22.5 8.9 %all-gather.1 = bf16[8,2,256]{2,1,0:T(2,128)(2,1)S(1)} all-gather(bf16[1,2,256]{2,1,0:T(2,128)(2,1)S(1)} %maximum_bitcast_fusion), channel_id=2, replica_groups=mesh['dp'=8,'tensor'=4] {'dp'}, dimensions={0}, use_global_device_ids=true | all-gather | bytes 9216 | tf_op jit(solution)/shard_map/all_gather | solution.py:292
  31.5 16.6 %collective-permute-done.1 = bf16[160,2048]{1,0:T(8,128)(2,1)S(1)} collective-permute-done((bf16[160,2048]{1,0:T(8,128)(2,1)S(1)}, bf16[160,2048]{1,0:T(8,128)(2,1)S(1)}, u32[]{:S(2)}, u32[]{:S(2)}) %collective-permute-start.1) | collective-permute-done | bytes 655392 | tf_op jit(solution)/shard_map/ppermute | solution.py:56
  49.9 15.2 %collective-permute-done.3 = bf16[160,2048]{1,0:T(8,128)(2,1)S(1)} collective-permute-done((bf16[160,2048]{1,0:T(8,128)(2,1)S(1)}, bf16[160,2048]{1,0:T(8,128)(2,1)S(1)}, u32[]{:S(2)}, u32[]{:S(2)}) %collective-permute-start.3) | collective-permute-done | bytes 655392 | tf_op jit(solution)/shard_map/ppermute | solution.py:60
  74.5 13.7 %shard_map.203 = (bf16[640,2048]{1,0:T(8,128)(2,1)S(1)}, bf16[640,2048]{1,0:T(8,128)(2,1)}, bf16[640,640]{1,0:T(8,128)(2,1)S(1)}, bf16[640,512]{1,0:T(8,128)(2,1)S(1)}, f32[8,640]{1,0:T(8,128)S(1)}) custom-call(bf16[640,2048]{1,0:T(8,128)(2,1)} %pad_maximum_fusion.1.x_ref, f32[1,2048]{1,0:T(1,128)S(1)} %bitcast.22, ...), custom_call_target="tpu_custom_call" | custom-call | flops 3858759680 | bytes 12582912 | tf_op jit(solution)/shard_map/pallas_call | solution.py:189
  92.4 19.0 %collective-permute-done.6 = bf16[160,2048]{1,0:T(8,128)(2,1)S(1)} collective-permute-done((bf16[160,2048]{1,0:T(8,128)(2,1)S(1)}, bf16[160,2048]{1,0:T(8,128)(2,1)S(1)}, u32[]{:S(2)}, u32[]{:S(2)}) %collective-permute-start.6) | collective-permute-done | bytes 655392 | tf_op jit(solution)/shard_map/ppermute | solution.py:56
  111.6 3.3 collective-permute-start.9
  116.9 26.3 %collective-permute-done.9 = bf16[160,2048]{1,0:T(8,128)(2,1)S(1)} collective-permute-done((bf16[160,2048]{1,0:T(8,128)(2,1)S(1)}, bf16[160,2048]{1,0:T(8,128)(2,1)S(1)}, u32[]{:S(2)}, u32[]{:S(2)}) %collective-permute-start.9) | collective-permute-done | bytes 655392 | tf_op jit(solution)/shard_map/ppermute | solution.py:56
  145.3 10.7 %collective-permute-done.11 = bf16[160,2048]{1,0:T(8,128)(2,1)S(1)} collective-permute-done((bf16[160,2048]{1,0:T(8,128)(2,1)S(1)}, bf16[160,2048]{1,0:T(8,128)(2,1)S(1)}, u32[]{:S(2)}, u32[]{:S(2)}) %collective-permute-start.11) | collective-permute-done | bytes 655392 | tf_op jit(solution)/shard_map/ppermute | solution.py:60
  162.5 25.0 %collective-permute-done.13 = bf16[160,2048]{1,0:T(8,128)(2,1)S(1)} collective-permute-done((bf16[160,2048]{1,0:T(8,128)(2,1)S(1)}, bf16[160,2048]{1,0:T(8,128)(2,1)S(1)}, u32[]{:S(2)}, u32[]{:S(2)}) %collective-permute-start.13) | collective-permute-done | bytes 655392 | tf_op jit(solution)/shard_map/ppermute | solution.py:56
  190.7 14.3 %collective-permute-done.15 = bf16[160,2048]{1,0:T(8,128)(2,1)S(1)} collective-permute-done((bf16[160,2048]{1,0:T(8,128)(2,1)S(1)}, bf16[160,2048]{1,0:T(8,128)(2,1)S(1)}, u32[]{:S(2)}, u32[]{:S(2)}) %collective-permute-start.15) | collective-permute-done | bytes 655392 | tf_op jit(solution)/shard_map/ppermute | solution.py:60
  205.9 13.8 %fusion.2 = f32[640,2816]{1,0:T(8,128)} fusion(bf16[2048,4224]{0,1:T(8,128)(2,1)} %all-gather.7.cloned.1.call-done, bf16[160,2048]{1,0:T(8,128)(2,1)} %broadcast_select_fusion.1, bf16[160,2048]{1,0:T(8,128)(2,1)} %copy-done.46, bf16[160,2048]{1,0:T(8,128)(2,1)} %collective-permute-done.12, bf16[160,2048]{1,0:T(8,128)(2,1)} %copy-done.27), kind=kOutput, calls=%fused_computation.2 | convolution fusion | flops 7392460800 | bytes 21364736 | tf_op jit(solution)/shard_map/dot_general | solution.py:35
  219.7 10.7 %multiply_convert_fusion.2 = (bf16[640,1408]{1,0:T(8,128)(2,1)S(1)}, bf16[640,1408]{1,0:T(8,128)(2,1)S(1)}, bf16[640,1408]{1,0:T(8,128)(2,1)S(1)}) fusion(f32[640,2816]{1,0:T(8,128)} %fusion.2, bf16[2048,4224]{0,1:T(8,128)(2,1)} %all-gather.7.cloned.1.call-done, bf16[160,2048]{1,0:T(8,128)(2,1)S(1)} %copy-done.31, bf16[160,2048]{1,0:T(8,128)(2,1)S(1)} %copy-done.40, ...), kind=kOutput, calls=%fused_computation.11 | convolution fusion | flops 3714990080 | bytes 21004288 | tf_op jit(solution)/shard_map/dot_general | solution.py:35
  230.4 11.3 %fusion.12 = bf16[640,2048]{1,0:T(8,128)(2,1)S(1)} fusion(bf16[2048,4224]{0,1:T(8,128)(2,1)} %all-gather.7.cloned.1.call-done, bf16[640,1408]{1,0:T(8,128)(2,1)S(1)} %get-tuple-element.205, bf16[640,1408]{1,0:T(8,128)(2,1)S(1)} %get-tuple-element.204), kind=kOutput, calls=%fused_computation.15 | convolution fusion | flops 7390494720 | bytes 17760256 | tf_op jit(solution)/shard_map/dot_general | solution.py:45
  246.2 11.9 %collective-permute-done.16 = bf16[160,2048]{1,0:T(8,128)(2,1)S(1)} collective-permute-done((bf16[160,2048]{1,0:T(8,128)(2,1)}, bf16[160,2048]{1,0:T(8,128)(2,1)S(1)}, u32[]{:S(2)}, u32[]{:S(2)}) %collective-permute-start.16) | collective-permute-done | bytes 655392 | tf_op jit(solution)/shard_map/ppermute | solution.py:64
  263.5 17.7 %shard_map.204 = bf16[2048,4224]{1,0:T(8,128)(2,1)} custom-call(bf16[640,2048]{1,0:T(8,128)(2,1)S(1)} %pad_maximum_fusion.3.refs_0_, bf16[640,2048]{1,0:T(8,128)(2,1)S(1)} %pad_maximum_fusion.2.refs_1_, bf16[640,2816]{1,0:T(8,128)(2,1)S(1)} %pad_maximum_fusion.refs_2_, bf16[640,1408]{1,0:T(8,128)(2,1)S(1)} %get-tuple-element.104.refs_3_), custom_call_target="tpu_custom_call" | custom-call | flops 11072962560 | bytes 27951104 | tf_op jit(solution)/shard_map/pallas_call | solution.py:120
  281.2 8.9 %fusion.9 = bf16[640,2048]{1,0:T(8,128)(2,1)} fusion(bf16[640,1408]{1,0:T(8,128)(2,1)} %copy-done.13, bf16[2048,4224]{0,1:T(8,128)(2,1)} %all-gather.7.cloned.1.call-done), kind=kOutput, calls=%fused_computation.14 | convolution fusion | flops 3692298240 | bytes 10190848 | tf_op jit(solution)/shard_map/dot_general | solution.py:45
  293.6 3.4 fusion.24
  297.7 13.5 %collective-permute-start.22 = (bf16[160,2048]{1,0:T(8,128)(2,1)S(1)}, bf16[160,2048]{1,0:T(8,128)(2,1)S(1)}, u32[]{:S(2)}, u32[]{:S(2)}) collective-permute-start(bf16[160,2048]{1,0:T(8,128)(2,1)S(1)} %get-tuple-element.200), channel_id=1, source_target_pairs={{0,2},{2,0},{1,3},{3,1},{4,6},{6,4},{5,7},{7,5},{8,10},{10,8},{9,1... | collective-permute-start | bytes 1966088 | tf_op jit(solution)/shard_map/ppermute | solution.py:56
  312.2 4.0 collective-permute-start.20
  316.2 36.1 %collective-permute-done.22 = bf16[160,2048]{1,0:T(8,128)(2,1)S(1)} collective-permute-done((bf16[160,2048]{1,0:T(8,128)(2,1)S(1)}, bf16[160,2048]{1,0:T(8,128)(2,1)S(1)}, u32[]{:S(2)}, u32[]{:S(2)}) %collective-permute-start.22) | collective-permute-done | bytes 655392 | tf_op jit(solution)/shard_map/ppermute | solution.py:56
  353.8 3.9 collective-permute-start.26
  358.4 27.4 %collective-permute-done.24 = bf16[160,2048]{1,0:T(8,128)(2,1)S(1)} collective-permute-done((bf16[160,2048]{1,0:T(8,128)(2,1)S(1)}, bf16[160,2048]{1,0:T(8,128)(2,1)S(1)}, u32[]{:S(2)}, u32[]{:S(2)}) %collective-permute-start.24) | collective-permute-done | bytes 655392 | tf_op jit(solution)/shard_map/ppermute | solution.py:60
  387.8 19.2 %shard_map.205 = (bf16[640,2048]{1,0:T(8,128)(2,1)}, bf16[640,640]{1,0:T(8,128)(2,1)}, f32[1,2048]{1,0:T(1,128)}) custom-call(bf16[640,2048]{1,0:T(8,128)(2,1)} %pad_maximum_fusion.4.g_ref.refs_1_, bf16[640,2048]{1,0:T(8,128)(2,1)} %pad_maximum_fusion.1.x_ref, f32[1,2048]{1,0:T(1,128)} %bitcast.23, bf16[2048,1152]{1,0:T(8,128)(2,1)} %all-gather.5.cloned.1.call-done.pack_ref, ...), custom_call_target="tpu_custom_call" | custom-call | flops 5117050880 | bytes 12582912 | tf_op jit(solution)/shard_map/pallas_call | solution.py:246
  407.0 3.8 fusion.25
  413.1 10.8 %collective-permute-done.28 = bf16[160,2048]{1,0:T(8,128)(2,1)S(1)} collective-permute-done((bf16[160,2048]{1,0:T(8,128)(2,1)S(1)}, bf16[160,2048]{1,0:T(8,128)(2,1)S(1)}, u32[]{:S(2)}, u32[]{:S(2)}) %collective-permute-start.28) | collective-permute-done | bytes 655392 | tf_op jit(solution)/shard_map/ppermute | solution.py:64
  424.9 4.8 collective-permute-start.31
  431.1 4.2 collective-permute-done.29
  440.4 6.3 %shard_map.206 = bf16[2048,1280]{1,0:T(8,128)(2,1)S(1)} custom-call(bf16[640,2048]{1,0:T(8,128)(2,1)S(1)} %copy-done.2, bf16[640,2048]{1,0:T(8,128)(2,1)S(1)} %copy-done.1, bf16[640,640]{1,0:T(8,128)(2,1)S(1)} %copy-done.3, bf16[640,512]{1,0:T(8,128)(2,1)S(1)} %copy-done.5, bf16[2048,128]{1,0:T(8,128)(2,1)S(1)} %pad.4.refs_4_), custom_call_target="tpu_custom_call" | custom-call | flops 3355443200 | bytes 12124160 | tf_op jit(solution)/shard_map/pallas_call | solution.py:120
  460.6 14.5 %collective-permute-done.33 = bf16[160,2048]{1,0:T(8,128)(2,1)} collective-permute-done((bf16[160,2048]{1,0:T(8,128)(2,1)}, bf16[160,2048]{1,0:T(8,128)(2,1)}, u32[]{:S(2)}, u32[]{:S(2)}) %collective-permute-start.33) | collective-permute-done | bytes 655392 | tf_op jit(solution)/shard_map/ppermute | solution.py:56
  479.9 3.1 fusion.21
  483.1 21.1 %reduce-scatter.5.cloned.1.call-done = bf16[256,1280]{1,0:T(8,128)(2,1)} async-done(((bf16[2048,1280]{1,0:T(8,128)(2,1)}), bf16[256,1280]{1,0:T(8,128)(2,1)}) %reduce-scatter.5.cloned.1.call-update) | async-done | bytes 655376 | tf_op jit(solution)/shard_map/reduce_scatter | solution.py:390
  (239 shorter events, 93.8 us)
Async XLA Ops:
  7.2 67.3 %all-gather.5.cloned.1.call-start = ((), (), s32[]{:S(2)}) async-start(), calls=%async_computation.2 | async-start | bytes 5308416 | tf_op jit(solution)/shard_map/all_gather | solution.py:289
  12.1 193.8 %all-gather.7.cloned.1.call-start = ((), (), s32[]{:S(2)}) async-start(), calls=%async_computation.3 | async-start | bytes 19464192 | tf_op jit(solution)/shard_map/all_gather | solution.py:297
  14.3 434.8 %reduce-scatter.3.cloned.1.call-start = ((), (), s32[]{:S(2)}) async-start(), calls=%async_computation.4 | async-start | bytes 19464192 | tf_op jit(solution)/shard_map/reduce_scatter | solution.py:349
  14.4 33.8 %collective-permute-start.1 = (bf16[160,2048]{1,0:T(8,128)(2,1)S(1)}, bf16[160,2048]{1,0:T(8,128)(2,1)S(1)}, u32[]{:S(2)}, u32[]{:S(2)}) collective-permute-start(bf16[160,2048]{1,0:T(8,128)(2,1)S(1)} %copy-done.19), channel_id=1, source_target_pairs={{0,2},{2,0},{1,3},{3,1},{4,6},{6,4},{5,7},{7,5},{8,10},{10,8},{9,1... | collective-permute-start | bytes 1966088 | tf_op jit(solution)/shard_map/ppermute | solution.py:56
  18.5 31.4 %collective-permute-start = (bf16[160,2048]{1,0:T(8,128)(2,1)S(1)}, bf16[160,2048]{1,0:T(8,128)(2,1)S(1)}, u32[]{:S(2)}, u32[]{:S(2)}) collective-permute-start(bf16[160,2048]{1,0:T(8,128)(2,1)S(1)} %copy-done.19), channel_id=1, source_target_pairs={{0,1},{1,0},{2,3},{3,2},{4,5},{5,4},{6,7},{7,6},{8,9},{9,8},{10,11... | collective-permute-start | bytes 1966088 | tf_op jit(solution)/shard_map/ppermute | solution.py:56
  20.1 29.8 %collective-permute-start.2 = (bf16[160,2048]{1,0:T(8,128)(2,1)S(1)}, bf16[160,2048]{1,0:T(8,128)(2,1)}, u32[]{:S(2)}, u32[]{:S(2)}) collective-permute-start(bf16[160,2048]{1,0:T(8,128)(2,1)S(1)} %copy-done.19), channel_id=1, source_target_pairs={{1,2},{2,1},{5,6},{6,5},{9,10},{10,9},{13,14},{14,13},{17,18},{18,... | collective-permute-start | bytes 1966088 | tf_op jit(solution)/shard_map/ppermute | solution.py:56
  65.1 27.3 %collective-permute-start.7 = (bf16[160,2048]{1,0:T(8,128)(2,1)S(1)}, bf16[160,2048]{1,0:T(8,128)(2,1)}, u32[]{:S(2)}, u32[]{:S(2)}) collective-permute-start(bf16[160,2048]{1,0:T(8,128)(2,1)S(1)} %copy-done.24), channel_id=1, source_target_pairs={{1,2},{2,1},{5,6},{6,5},{9,10},{10,9},{13,14},{14,13},{17,18},{18,... | collective-permute-start | bytes 1966088 | tf_op jit(solution)/shard_map/ppermute | solution.py:56
  66.8 44.5 %collective-permute-start.6 = (bf16[160,2048]{1,0:T(8,128)(2,1)S(1)}, bf16[160,2048]{1,0:T(8,128)(2,1)S(1)}, u32[]{:S(2)}, u32[]{:S(2)}) collective-permute-start(bf16[160,2048]{1,0:T(8,128)(2,1)S(1)} %copy-done.24), channel_id=1, source_target_pairs={{0,2},{2,0},{1,3},{3,1},{4,6},{6,4},{5,7},{7,5},{8,10},{10,8},{9,1... | collective-permute-start | bytes 1966088 | tf_op jit(solution)/shard_map/ppermute | solution.py:56
  69.6 41.7 %collective-permute-start.5 = (bf16[160,2048]{1,0:T(8,128)(2,1)S(1)}, bf16[160,2048]{1,0:T(8,128)(2,1)}, u32[]{:S(2)}, u32[]{:S(2)}) collective-permute-start(bf16[160,2048]{1,0:T(8,128)(2,1)S(1)} %copy-done.24), channel_id=1, source_target_pairs={{0,1},{1,0},{2,3},{3,2},{4,5},{5,4},{6,7},{7,6},{8,9},{9,8},{10,11... | collective-permute-start | bytes 1966088 | tf_op jit(solution)/shard_map/ppermute | solution.py:56
  89.3 22.1 %collective-permute-start.4 = (bf16[160,2048]{1,0:T(8,128)(2,1)S(1)}, bf16[160,2048]{1,0:T(8,128)(2,1)S(1)}, u32[]{:S(2)}, u32[]{:S(2)}) collective-permute-start(bf16[160,2048]{1,0:T(8,128)(2,1)S(1)} %get-tuple-element.86), channel_id=1, source_target_pairs={{0,1},{3,2},{4,5},{7,6},{8,9},{11,10},{12,13},{15,14},{16,17},{19,... | collective-permute-start | bytes 1966088 | tf_op jit(solution)/shard_map/ppermute | solution.py:64
  111.6 31.7 %collective-permute-start.9 = (bf16[160,2048]{1,0:T(8,128)(2,1)S(1)}, bf16[160,2048]{1,0:T(8,128)(2,1)S(1)}, u32[]{:S(2)}, u32[]{:S(2)}) collective-permute-start(bf16[160,2048]{1,0:T(8,128)(2,1)S(1)} %add_convert_fusion.4), channel_id=1, source_target_pairs={{0,2},{2,0},{1,3},{3,1},{4,6},{6,4},{5,7},{7,5},{8,10},{10,8},{9,1... | collective-permute-start | bytes 1966088 | tf_op jit(solution)/shard_map/ppermute | solution.py:56
  114.9 30.4 %collective-permute-start.8 = (bf16[160,2048]{1,0:T(8,128)(2,1)S(1)}, bf16[160,2048]{1,0:T(8,128)(2,1)S(1)}, u32[]{:S(2)}, u32[]{:S(2)}) collective-permute-start(bf16[160,2048]{1,0:T(8,128)(2,1)S(1)} %get-tuple-element.83), channel_id=1, source_target_pairs={{0,1},{1,0},{2,3},{3,2},{4,5},{5,4},{6,7},{7,6},{8,9},{9,8},{10,11... | collective-permute-start | bytes 1966088 | tf_op jit(solution)/shard_map/ppermute | solution.py:56
  114.9 30.4 %collective-permute-start.10 = (bf16[160,2048]{1,0:T(8,128)(2,1)S(1)}, bf16[160,2048]{1,0:T(8,128)(2,1)S(1)}, u32[]{:S(2)}, u32[]{:S(2)}) collective-permute-start(bf16[160,2048]{1,0:T(8,128)(2,1)S(1)} %get-tuple-element.86), channel_id=1, source_target_pairs={{1,2},{2,1},{5,6},{6,5},{9,10},{10,9},{13,14},{14,13},{17,18},{18,... | collective-permute-start | bytes 1966088 | tf_op jit(solution)/shard_map/ppermute | solution.py:56
  115.6 40.5 %collective-permute-start.11 = (bf16[160,2048]{1,0:T(8,128)(2,1)S(1)}, bf16[160,2048]{1,0:T(8,128)(2,1)S(1)}, u32[]{:S(2)}, u32[]{:S(2)}) collective-permute-start(bf16[160,2048]{1,0:T(8,128)(2,1)S(1)} %collective-permute-done.6), channel_id=1, source_target_pairs={{1,0},{2,3},{5,4},{6,7},{9,8},{10,11},{13,12},{14,15},{17,16},{18,... | collective-permute-start | bytes 1966088 | tf_op jit(solution)/shard_map/ppermute | solution.py:60
  157.0 30.5 %collective-permute-start.13 = (bf16[160,2048]{1,0:T(8,128)(2,1)S(1)}, bf16[160,2048]{1,0:T(8,128)(2,1)S(1)}, u32[]{:S(2)}, u32[]{:S(2)}) collective-permute-start(bf16[160,2048]{1,0:T(8,128)(2,1)S(1)} %multiply_convert_fusion.3), channel_id=1, source_target_pairs={{0,2},{2,0},{1,3},{3,1},{4,6},{6,4},{5,7},{7,5},{8,10},{10,8},{9,1... | collective-permute-start | bytes 1966088 | tf_op jit(solution)/shard_map/ppermute | solution.py:56
  158.7 31.9 %collective-permute-start.14 = (bf16[160,2048]{1,0:T(8,128)(2,1)S(1)}, bf16[160,2048]{1,0:T(8,128)(2,1)S(1)}, u32[]{:S(2)}, u32[]{:S(2)}) collective-permute-start(bf16[160,2048]{1,0:T(8,128)(2,1)S(1)} %multiply_convert_fusion.3), channel_id=1, source_target_pairs={{1,2},{2,1},{5,6},{6,5},{9,10},{10,9},{13,14},{14,13},{17,18},{18,... | collective-permute-start | bytes 1966088 | tf_op jit(solution)/shard_map/ppermute | solution.py:56
  159.4 46.4 %collective-permute-start.12 = (bf16[160,2048]{1,0:T(8,128)(2,1)S(1)}, bf16[160,2048]{1,0:T(8,128)(2,1)}, u32[]{:S(2)}, u32[]{:S(2)}) collective-permute-start(bf16[160,2048]{1,0:T(8,128)(2,1)S(1)} %multiply_convert_fusion.3), channel_id=1, source_target_pairs={{0,1},{1,0},{2,3},{3,2},{4,5},{5,4},{6,7},{7,6},{8,9},{9,8},{10,11... | collective-permute-start | bytes 1966088 | tf_op jit(solution)/shard_map/ppermute | solution.py:56
  259.1 31.0 %collective-permute-start.18 = (bf16[160,2048]{1,0:T(8,128)(2,1)}, bf16[160,2048]{1,0:T(8,128)(2,1)}, u32[]{:S(2)}, u32[]{:S(2)}) collective-permute-start(bf16[160,2048]{1,0:T(8,128)(2,1)} %add_convert_fusion.3), channel_id=1, source_target_pairs={{0,2},{2,0},{1,3},{3,1},{4,6},{6,4},{5,7},{7,5},{8,10},{10,8},{9,1... | collective-permute-start | bytes 1966088 | tf_op jit(solution)/shard_map/ppermute | solution.py:56
  259.1 31.0 %collective-permute-start.17 = (bf16[160,2048]{1,0:T(8,128)(2,1)}, bf16[160,2048]{1,0:T(8,128)(2,1)}, u32[]{:S(2)}, u32[]{:S(2)}) collective-permute-start(bf16[160,2048]{1,0:T(8,128)(2,1)} %get-tuple-element.99), channel_id=1, source_target_pairs={{0,1},{1,0},{2,3},{3,2},{4,5},{5,4},{6,7},{7,6},{8,9},{9,8},{10,11... | collective-permute-start | bytes 1966088 | tf_op jit(solution)/shard_map/ppermute | solution.py:56
  261.5 28.6 %collective-permute-start.19 = (bf16[160,2048]{1,0:T(8,128)(2,1)}, bf16[160,2048]{1,0:T(8,128)(2,1)}, u32[]{:S(2)}, u32[]{:S(2)}) collective-permute-start(bf16[160,2048]{1,0:T(8,128)(2,1)} %get-tuple-element.102), channel_id=1, source_target_pairs={{1,2},{2,1},{5,6},{6,5},{9,10},{10,9},{13,14},{14,13},{17,18},{18,... | collective-permute-start | bytes 1966088 | tf_op jit(solution)/shard_map/ppermute | solution.py:56
  290.2 214.0 %reduce-scatter.5.cloned.1.call-start = ((), (), s32[]{:S(2)}) async-start(), calls=%async_computation.5 | async-start | bytes 5898240 | tf_op jit(solution)/shard_map/reduce_scatter | solution.py:390
  297.0 19.2 %collective-permute-start.23 = (bf16[160,2048]{1,0:T(8,128)(2,1)S(1)}, bf16[160,2048]{1,0:T(8,128)(2,1)S(1)}, u32[]{:S(2)}, u32[]{:S(2)}) collective-permute-start(bf16[160,2048]{1,0:T(8,128)(2,1)S(1)} %get-tuple-element.200), channel_id=1, source_target_pairs={{1,2},{2,1},{5,6},{6,5},{9,10},{10,9},{13,14},{14,13},{17,18},{18,... | collective-permute-start | bytes 1966088 | tf_op jit(solution)/shard_map/ppermute | solution.py:56
  297.7 54.6 %collective-permute-start.22 = (bf16[160,2048]{1,0:T(8,128)(2,1)S(1)}, bf16[160,2048]{1,0:T(8,128)(2,1)S(1)}, u32[]{:S(2)}, u32[]{:S(2)}) collective-permute-start(bf16[160,2048]{1,0:T(8,128)(2,1)S(1)} %get-tuple-element.200), channel_id=1, source_target_pairs={{0,2},{2,0},{1,3},{3,1},{4,6},{6,4},{5,7},{7,5},{8,10},{10,8},{9,1... | collective-permute-start | bytes 1966088 | tf_op jit(solution)/shard_map/ppermute | solution.py:56
  311.2 41.1 %collective-permute-start.21 = (bf16[160,2048]{1,0:T(8,128)(2,1)S(1)}, bf16[160,2048]{1,0:T(8,128)(2,1)S(1)}, u32[]{:S(2)}, u32[]{:S(2)}) collective-permute-start(bf16[160,2048]{1,0:T(8,128)(2,1)S(1)} %get-tuple-element.200), channel_id=1, source_target_pairs={{0,1},{1,0},{2,3},{3,2},{4,5},{5,4},{6,7},{7,6},{8,9},{9,8},{10,11... | collective-permute-start | bytes 1966088 | tf_op jit(solution)/shard_map/ppermute | solution.py:56
  312.2 40.1 %collective-permute-start.20 = (bf16[160,2048]{1,0:T(8,128)(2,1)S(1)}, bf16[160,2048]{1,0:T(8,128)(2,1)S(1)}, u32[]{:S(2)}, u32[]{:S(2)}) collective-permute-start(bf16[160,2048]{1,0:T(8,128)(2,1)S(1)} %get-tuple-element.120), channel_id=1, source_target_pairs={{0,1},{3,2},{4,5},{7,6},{8,9},{11,10},{12,13},{15,14},{16,17},{19,... | collective-permute-start | bytes 1966088 | tf_op jit(solution)/shard_map/ppermute | solution.py:64
  352.3 33.5 %collective-permute-start.24 = (bf16[160,2048]{1,0:T(8,128)(2,1)S(1)}, bf16[160,2048]{1,0:T(8,128)(2,1)S(1)}, u32[]{:S(2)}, u32[]{:S(2)}) collective-permute-start(bf16[160,2048]{1,0:T(8,128)(2,1)S(1)} %collective-permute-done.22), channel_id=1, source_target_pairs={{1,0},{2,3},{5,4},{6,7},{9,8},{10,11},{13,12},{14,15},{17,16},{18,... | collective-permute-start | bytes 1966088 | tf_op jit(solution)/shard_map/ppermute | solution.py:60
  353.8 53.1 %collective-permute-start.26 = (bf16[160,2048]{1,0:T(8,128)(2,1)S(1)}, bf16[160,2048]{1,0:T(8,128)(2,1)S(1)}, u32[]{:S(2)}, u32[]{:S(2)}) collective-permute-start(bf16[160,2048]{1,0:T(8,128)(2,1)S(1)} %add_convert_fusion.2), channel_id=1, source_target_pairs={{0,2},{2,0},{1,3},{3,1},{4,6},{6,4},{5,7},{7,5},{8,10},{10,8},{9,1... | collective-permute-start | bytes 1966088 | tf_op jit(solution)/shard_map/ppermute | solution.py:56
  357.7 49.2 %collective-permute-start.25 = (bf16[160,2048]{1,0:T(8,128)(2,1)S(1)}, bf16[160,2048]{1,0:T(8,128)(2,1)S(1)}, u32[]{:S(2)}, u32[]{:S(2)}) collective-permute-start(bf16[160,2048]{1,0:T(8,128)(2,1)S(1)} %get-tuple-element.117), channel_id=1, source_target_pairs={{0,1},{1,0},{2,3},{3,2},{4,5},{5,4},{6,7},{7,6},{8,9},{9,8},{10,11... | collective-permute-start | bytes 1966088 | tf_op jit(solution)/shard_map/ppermute | solution.py:56
  357.7 49.2 %collective-permute-start.27 = (bf16[160,2048]{1,0:T(8,128)(2,1)S(1)}, bf16[160,2048]{1,0:T(8,128)(2,1)S(1)}, u32[]{:S(2)}, u32[]{:S(2)}) collective-permute-start(bf16[160,2048]{1,0:T(8,128)(2,1)S(1)} %get-tuple-element.120), channel_id=1, source_target_pairs={{1,2},{2,1},{5,6},{6,5},{9,10},{10,9},{13,14},{14,13},{17,18},{18,... | collective-permute-start | bytes 1966088 | tf_op jit(solution)/shard_map/ppermute | solution.py:56
  429.7 19.4 %collective-permute-start.32 = (bf16[160,2048]{1,0:T(8,128)(2,1)}, bf16[160,2048]{1,0:T(8,128)(2,1)}, u32[]{:S(2)}, u32[]{:S(2)}) collective-permute-start(bf16[160,2048]{1,0:T(8,128)(2,1)} %get-tuple-element.134), channel_id=1, source_target_pairs={{0,1},{1,0},{2,3},{3,2},{4,5},{5,4},{6,7},{7,6},{8,9},{9,8},{10,11... | collective-permute-start | bytes 1966088 | tf_op jit(solution)/shard_map/ppermute | solution.py:56
  451.4 23.7 %collective-permute-start.33 = (bf16[160,2048]{1,0:T(8,128)(2,1)}, bf16[160,2048]{1,0:T(8,128)(2,1)}, u32[]{:S(2)}, u32[]{:S(2)}) collective-permute-start(bf16[160,2048]{1,0:T(8,128)(2,1)} %add_convert_fusion), channel_id=1, source_target_pairs={{0,2},{2,0},{1,3},{3,1},{4,6},{6,4},{5,7},{7,5},{8,10},{10,8},{9,1... | collective-permute-start | bytes 1966088 | tf_op jit(solution)/shard_map/ppermute | solution.py:56
  451.4 23.7 %collective-permute-start.34 = (bf16[160,2048]{1,0:T(8,128)(2,1)}, bf16[160,2048]{1,0:T(8,128)(2,1)}, u32[]{:S(2)}, u32[]{:S(2)}) collective-permute-start(bf16[160,2048]{1,0:T(8,128)(2,1)} %copy-done.43), channel_id=1, source_target_pairs={{1,2},{2,1},{5,6},{6,5},{9,10},{10,9},{13,14},{14,13},{17,18},{18,... | collective-permute-start | bytes 1966088 | tf_op jit(solution)/shard_map/ppermute | solution.py:56
  (61 other events, 808.2 us)
Sparse Core Ops, SparseCore 0:
  12.2 41.6 all-gather.4
  55.8 95.4 all-gather.6
  290.3 128.3 reduce-scatter.2
  449.2 54.9 reduce-scatter.4
